TPU v7x, 128 devices: a whole 4x4x4 slice. The times are simulated.
128 devices in a mesh: leaf: 32 (over y, z, core), sub: 4 (over x).
Axes of the slice: x: 4, y: 4, z: 4, core: 2. Of those that a mesh axis runs over, the one named last changes fastest.
Arguments:
- points: float32 [3, 131072], P(None, ('leaf', 'sub')), may hold values from 0 to 4
- order: int32 [128, 1024], P(('leaf', 'sub')), may hold values from 0 to 1023, each once within a row
- counts: int32 [128], P(('leaf', 'sub')), may hold values from 1 to 1024, 98304 in all
- basis: float32 [131072, 896], P(('leaf', 'sub')), may hold values from -0.1875 to 0.1875
- right_side: float32 [131072, 128], P(('leaf', 'sub')), may hold values from -6 to 6
- coupling: float32 [7, 256, 256], replicated, may hold values from -0.375 to 0.375
Outputs:
- solution: float32 [131072, 128], P(('leaf', 'sub'))
Inputs may be any that keep to these rules, and one draw needn't show every extreme that they name: `order`: each row orders the 1024 slots of one leaf, every slot once. `counts`: slots of a leaf at or past its count are padding; some leaf is full.
All inputs are finite; a program needn't handle non-finite values. No bound on the sum of `counts` on one device may be relied on, other than what follows from the above.
Results may differ from a plain program's by a relative error of at most 0.0003.
Values sent between devices are 32-bit elements; how exact they have to be, the bound alone decides.
A program may use at most 128 MiB of HBM per device.

v0:
```python
import jax
import jax.numpy as jnp
from jax import lax
from jax.sharding import PartitionSpec as P

R = 128


GAMMA_RATE = 2.0
NUGGET_VALUE = 1.0


def swapped(shard, axis, stride):
    return lax.ppermute(shard, axis, [(i, i ^ 1 << stride) for i in range(lax.axis_size(axis))])


def leaf_solve(coords, ordering, count, basis_rows, rhs_rows):
    ordered = coords[:, ordering]
    live_mask = (jnp.arange(coords.shape[1]) < count).astype(jnp.float32)
    offsets = ordered[:, :, None] - ordered[:, None, :]
    distance = jnp.sum(offsets * offsets, axis=0)
    kernel = jnp.exp(-GAMMA_RATE * distance) * live_mask[:, None] * live_mask[None, :]
    kernel = kernel + NUGGET_VALUE * jnp.eye(coords.shape[1], dtype=jnp.float32)
    lower_tri = jnp.linalg.cholesky(kernel)
    stacked = jnp.concatenate([basis_rows, rhs_rows], axis=1) * live_mask[:, None]
    solved = jax.scipy.linalg.cho_solve((lower_tri, True), stacked)
    return (solved, stacked[:, : basis_rows.shape[1]])


def couple(first_sums, second_sums, factor):
    upper_half = factor[:R]
    lower_half = factor[R:]
    highest = lax.Precision.HIGHEST
    first_block = first_sums[:, :R]
    second_block = second_sums[:, :R]
    coupled = jnp.eye(2 * R, dtype=jnp.float32)
    coupled = coupled + jnp.dot(
        upper_half.T, jnp.dot(first_block, upper_half, precision=highest), precision=highest
    )
    coupled = coupled + jnp.dot(
        lower_half.T, jnp.dot(second_block, lower_half, precision=highest), precision=highest
    )
    coupled = 0.5 * (coupled + coupled.T)
    forcing = jnp.dot(upper_half.T, first_sums, precision=highest) + jnp.dot(
        lower_half.T, second_sums, precision=highest
    )
    lower_tri = jnp.linalg.cholesky(coupled)
    solved_coef = jax.scipy.linalg.cho_solve((lower_tri, True), forcing)
    return jnp.dot(factor, solved_coef, precision=highest)


def pair_swap(payload, bit_index, sub_bits):
    if bit_index < sub_bits:
        return swapped(payload, "sub", bit_index)
    return swapped(payload, "leaf", bit_index - sub_bits)


def shards(points, order, counts, basis, right_side, coupling):
    highest = lax.Precision.HIGHEST
    solved, masked = leaf_solve(points, order[0], counts[0], basis, right_side)
    levels = basis.shape[1] // R
    sub_bits = lax.axis_size("sub").bit_length() - 1
    position = lax.axis_index("leaf") * lax.axis_size("sub") + lax.axis_index("sub")
    for tree_level in range(levels):
        col_start = tree_level * R
        own_sums = jnp.einsum(
            "nr,nc->rc",
            masked[:, col_start : col_start + R],
            solved[:, col_start:],
            precision=highest,
        )
        lowest = 0
        if tree_level >= sub_bits:
            lowest = 0
        for bit_index in range(lowest, tree_level):
            own_sums = own_sums + pair_swap(own_sums, bit_index, sub_bits)
        sibling = pair_swap(own_sums, tree_level, sub_bits)
        side_bit = position >> tree_level & 1
        first_sums = jnp.where(side_bit == 0, own_sums, sibling)
        second_sums = jnp.where(side_bit == 0, sibling, own_sums)
        mixed = couple(first_sums, second_sums, coupling[tree_level])
        own_mixed = jnp.where(side_bit == 0, mixed[:R], mixed[R:])
        update = jnp.dot(solved[:, col_start : col_start + R], own_mixed, precision=highest)
        solved = solved.at[:, col_start:].add(-update)
    return solved[:, levels * R :]


def solution(mesh):
    placed = (
        P(None, ("leaf", "sub")),
        P(("leaf", "sub"), None),
        P(("leaf", "sub")),
        P(("leaf", "sub"), None),
        P(("leaf", "sub"), None),
        P(),
    )
    return jax.shard_map(
        shards, mesh=mesh, in_specs=placed, out_specs=P(("leaf", "sub"), None), check_vma=False
    )
```

profile of v0, /device:TPU:0, one launch (start us, length us, event | category | flops | bytes accessed | tf_op | source)
XLA Modules:
  0.0 1212.3 jit_solution(1839965613445632300)
XLA Ops:
  37.9 11.7 cholesky.253
  49.7 9.8 custom-call.117
  65.9 11.9 cholesky.276
  78.4 9.8 custom-call.118
  91.6 11.7 cholesky.301
  104.7 9.8 custom-call.119
  118.0 12.1 cholesky.543
  131.5 9.8 custom-call.120
  144.8 11.7 cholesky.562
  157.8 10.0 custom-call.121
  171.1 11.7 cholesky.582
  184.1 9.8 custom-call.122
  197.0 11.9 cholesky.602
  210.1 9.8 custom-call.145
  222.6 11.7 cholesky.616
  246.3 22.5 %while.16 = (s32[]{:T(128)}, f32[1024,1024]{1,0:T(8,128)}, s32[8,2]{0,1:T(2,128)S(1)}, f32[8,128,128]{2,1,0:T(8,128)S(1)}, s32[]{:T(128)}) while((s32[]{:T(128)}, f32[1024,1024]{1,0:T(8,128)}, s32[8,2]{0,1:T(2,128)S(1)}, f32[8,128,128]{2,1,0:T(8,128)S(1)}, s32[]{:T(128)}) %tuple.216), condition=%wide.while_cond.7, body=%wide.while_body.7.sunk | while | flops 2 | bytes 131181 | solution.py:26
  268.8 79.0 %custom-call.123 = f32[8,128,128]{1,2,0:T(8,128)S(1)} custom-call(f32[8,128,128]{2,1,0:T(8,128)S(1)} %get-tuple-element.106), custom_call_target="InvertDiagBlocksLowerTriangular" | custom-call | tf_op jit(solution)/shard_map/jit(_cho_solve)/triangular_solve | solution.py:26
  402.4 11.9 collective-permute-done
  427.4 11.7 cholesky.846
  439.9 9.8 custom-call.146
  452.5 12.1 cholesky.856
  475.6 20.5 %custom-call.124 = f32[2,128,128]{1,2,0:T(8,128)S(1)} custom-call(f32[2,128,128]{2,1,0:T(8,128)} %copy-done.27), custom_call_target="InvertDiagBlocksLowerTriangular" | custom-call | tf_op jit(solution)/shard_map/jit(_cho_solve)/triangular_solve | solution.py:48
  515.2 9.6 collective-permute-done.1
  544.9 11.7 cholesky.873
  557.2 10.6 custom-call.147
  570.7 12.9 %cholesky.883 = f32[128,128]{1,0:T(8,128)S(1)} custom-call(f32[128,128]{1,0:T(8,128)} %convolution_subtract_fusion.28), custom_call_target="Cholesky" | custom-call | tf_op jit(solution)/shard_map/jit(cholesky)/cholesky | solution.py:47
  593.1 21.1 %custom-call.125 = f32[2,128,128]{1,2,0:T(8,128)} custom-call(f32[2,128,128]{2,1,0:T(8,128)} %get-tuple-element.122), custom_call_target="InvertDiagBlocksLowerTriangular" | custom-call | tf_op jit(solution)/shard_map/jit(_cho_solve)/triangular_solve | solution.py:48
  658.3 11.7 cholesky.900
  670.0 9.8 custom-call.148
  682.0 12.1 cholesky.910
  700.8 19.7 %custom-call.126 = f32[2,128,128]{1,2,0:T(8,128)S(1)} custom-call(f32[2,128,128]{2,1,0:T(8,128)S(1)} %get-tuple-element.130), custom_call_target="InvertDiagBlocksLowerTriangular" | custom-call | tf_op jit(solution)/shard_map/jit(_cho_solve)/triangular_solve | solution.py:48
  736.0 9.0 collective-permute-done.6
  772.4 11.7 cholesky.927
  784.2 9.8 custom-call.149
  796.2 12.1 cholesky.937
  815.1 19.7 %custom-call.127 = f32[2,128,128]{1,2,0:T(8,128)S(1)} custom-call(f32[2,128,128]{2,1,0:T(8,128)S(1)} %get-tuple-element.138), custom_call_target="InvertDiagBlocksLowerTriangular" | custom-call | tf_op jit(solution)/shard_map/jit(_cho_solve)/triangular_solve | solution.py:48
  888.4 11.7 cholesky.954
  900.2 9.8 custom-call.150
  910.4 11.9 cholesky.964
  929.3 19.7 %custom-call.128 = f32[2,128,128]{1,2,0:T(8,128)S(1)} custom-call(f32[2,128,128]{2,1,0:T(8,128)S(1)} %get-tuple-element.146), custom_call_target="InvertDiagBlocksLowerTriangular" | custom-call | tf_op jit(solution)/shard_map/jit(_cho_solve)/triangular_solve | solution.py:48
  999.7 11.7 cholesky.981
  1011.5 9.8 custom-call.151
  1021.8 11.7 cholesky.991
  1040.3 19.7 %custom-call.129 = f32[2,128,128]{1,2,0:T(8,128)S(1)} custom-call(f32[2,128,128]{2,1,0:T(8,128)S(1)} %get-tuple-element.154), custom_call_target="InvertDiagBlocksLowerTriangular" | custom-call | tf_op jit(solution)/shard_map/jit(_cho_solve)/triangular_solve | solution.py:48
  1122.6 13.2 %cholesky.1008 = f32[128,128]{1,0:T(8,128)} custom-call(f32[128,128]{1,0:T(8,128)} %cholesky.1082), custom_call_target="Cholesky" | custom-call | tf_op jit(solution)/shard_map/jit(cholesky)/cholesky | solution.py:47
  1138.8 11.3 custom-call.152
  1153.5 13.4 %cholesky.1018 = f32[128,128]{1,0:T(8,128)} custom-call(f32[128,128]{1,0:T(8,128)} %convolution_subtract_fusion.23), custom_call_target="Cholesky" | custom-call | tf_op jit(solution)/shard_map/jit(cholesky)/cholesky | solution.py:47
  1180.3 21.1 %custom-call.130 = f32[2,128,128]{1,2,0:T(8,128)} custom-call(f32[2,128,128]{2,1,0:T(8,128)} %get-tuple-element.162), custom_call_target="InvertDiagBlocksLowerTriangular" | custom-call | tf_op jit(solution)/shard_map/jit(_cho_solve)/triangular_solve | solution.py:48
  (530 shorter events, 574.1 us)
Async XLA Ops:
  13.8 5.1 copy-start.25
  35.9 2.0 copy-start.7
  347.8 4.8 copy-start
  351.8 4.6 copy-start.4
  398.1 2.4 copy-start.9
  398.1 16.3 %copy-start.1 = (f32[7,256,256]{2,1,0:T(8,128)S(1)}, f32[7,256,256]{2,1,0:T(8,128)}, u32[]{:S(2)}) copy-start(f32[7,256,256]{2,1,0:T(8,128)} %param.30) | copy-start | bytes 5505028
  400.6 13.7 %collective-permute-start = (f32[128,1024]{1,0:T(8,128)S(1)}, f32[128,1024]{1,0:T(8,128)S(1)}, u32[]{:S(2)}, u32[]{:S(2)}) collective-permute-start(f32[128,1024]{1,0:T(8,128)S(1)} %fusion.101), channel_id=1, source_target_pairs={{0,1},{1,0},{2,3},{3,2},{4,5},{5,4},{6,7},{7,6},{8,9},{9,8},{10,11... | collective-permute-start | bytes 1572872 | tf_op jit(solution)/shard_map/ppermute | solution.py:14
  496.1 1.7 copy-start.13
  508.1 2.0 copy-start.2
  513.4 11.5 collective-permute-start.1
  524.9 12.2 %collective-permute-start.2 = (f32[128,896]{1,0:T(8,128)S(1)}, f32[128,896]{1,0:T(8,128)S(1)}, u32[]{:S(2)}, u32[]{:S(2)}) collective-permute-start(f32[128,896]{1,0:T(8,128)S(1)} %add.429), channel_id=1, source_target_pairs={{0,2},{1,3},{2,0},{3,1},{4,6},{5,7},{6,4},{7,5},{8,10},{9,11},{10,... | collective-permute-start | bytes 1376264 | tf_op jit(solution)/shard_map/ppermute | solution.py:14
  537.2 1.2 copy-start.11
  542.3 71.9 %copy-start.12 = (f32[128,896]{1,0:T(8,128)S(1)}, f32[128,896]{1,0:T(8,128)}, u32[]{:S(2)}) copy-start(f32[128,896]{1,0:T(8,128)} %copy-done.11) | copy-start | bytes 1376260
  583.6 2.5 copy-start.18
  614.2 3.3 copy-start.26
  626.4 1.8 copy-start.3
  631.2 8.2 collective-permute-start.3
  639.5 10.8 collective-permute-start.4
  650.3 2.0 collective-permute-start.5
  657.4 63.2 %copy-start.15 = (f32[128,768]{1,0:T(8,128)S(1)}, f32[128,768]{1,0:T(8,128)}, u32[]{:S(2)}) copy-start(f32[128,768]{1,0:T(8,128)} %copy-done.14) | copy-start | bytes 1179652
  730.5 1.7 copy-start.5
  734.9 10.0 collective-permute-start.6
  745.0 10.8 collective-permute-start.7
  755.8 1.7 collective-permute-start.8
  757.5 9.8 collective-permute-start.9
  771.5 63.3 %copy-start.17 = (f32[128,640]{1,0:T(8,128)S(1)}, f32[128,640]{1,0:T(8,128)}, u32[]{:S(2)}) copy-start(f32[128,640]{1,0:T(8,128)} %copy-done.16) | copy-start | bytes 983044
  843.7 1.5 copy-start.6
  847.6 7.6 collective-permute-start.10
  855.2 8.2 collective-permute-start.11
  863.5 1.6 collective-permute-start.12
  865.1 8.4 collective-permute-start.13
  873.6 9.7 collective-permute-start.14
  956.5 1.3 copy-start.8
  960.0 5.7 collective-permute-start.15
  965.8 7.3 collective-permute-start.16
  973.1 1.5 collective-permute-start.17
  974.6 7.0 collective-permute-start.18
  981.7 7.7 collective-permute-start.19
  989.4 6.2 collective-permute-start.20
  1068.1 5.0 collective-permute-start.21
  1073.2 7.4 collective-permute-start.22
  1080.6 1.4 collective-permute-start.23
  1082.1 5.6 collective-permute-start.24
  1087.7 6.7 collective-permute-start.25
  1094.4 5.0 collective-permute-start.26
  1099.5 4.7 copy-start.24
  1099.5 6.9 collective-permute-start.27
  1201.4 9.8 copy-start.10
  (8 other events, 6.3 us)
where the time goes:
time: 1220 us; the launch traced here: 1210 us
  other arithmetic  687 us (56%)
  matrix products  190 us (16%)
  waiting for transfers between devices  141 us (12%)
  local copies, waits for them, and re-layouts  119 us (10%)
  starting transfers between devices  57.8 us (5%)
  between operations  17.2 us (1%)
    another operation x49, other arithmetic, couple(): lower_tri = jnp.linalg.cholesky(coupled)  255 us
    another operation x30, other arithmetic, leaf_solve(): lower_tri = jnp.linalg.cholesky(kernel)  173 us
    another operation x15, other arithmetic, couple(): solved_coef = jax.scipy.linalg.cho_solve((lower_tri, True), forcing)  146 us
    ppermute x28, waiting for transfers between devices, swapped(): lax.ppermute(shard, axis, [(i, i ^ 1 << stride) for i in range(lax.axis_s...  141 us
    another operation x3, other arithmetic, leaf_solve(): solved = jax.scipy.linalg.cho_solve((lower_tri, True), stacked)  83.8 us
    ppermute x28, starting transfers between devices, swapped(): lax.ppermute(shard, axis, [(i, i ^ 1 << stride) for i in range(lax.axis_s...  57.8 us
    another operation x67, local copies, waits for them, and re-layouts  57.1 us
    another operation x30, matrix products, leaf_solve(): solved = jax.scipy.linalg.cho_solve((lower_tri, True), stacked)  49.1 us
  transfers between devices with their start and end apart: 28, of which 28 were waited for; matrix products, arithmetic and copies ran while one was open for 0% of the time, Pallas kernels for 0%

commit v1 on v0

v1 whole, which is shorter than its diff:
```python
import functools

import jax
import jax.numpy as jnp
from jax import lax
from jax.experimental import pallas as pl
from jax.experimental.pallas import tpu as pltpu
from jax.sharding import PartitionSpec as P

R = 128
GAMMA_RATE = 2.0
NUGGET_VALUE = 1.0
F32 = jnp.float32
BF16 = jnp.bfloat16
VMEM = pl.BlockSpec(memory_space=pltpu.VMEM)
SMEM = pl.BlockSpec(memory_space=pltpu.SMEM)
PARAMS = pltpu.CompilerParams(vmem_limit_bytes=56 * 1024 * 1024)


def split(x):
    high = x.astype(BF16)
    low = (x - high.astype(F32)).astype(BF16)
    return high, low


def dot(a, b):
    return jnp.dot(a, b, preferred_element_type=F32)


def wide(x):
    high, low = split(x)
    return jnp.concatenate([high, high, low], axis=1)


def tall(x):
    high, low = split(x)
    return jnp.concatenate([high, low, high], axis=0)


def dot3(a, b):
    return dot(wide(a), tall(b))


def identity(n):
    rows = lax.broadcasted_iota(jnp.int32, (n, n), 0)
    cols = lax.broadcasted_iota(jnp.int32, (n, n), 1)
    return (rows == cols).astype(F32)


def factor(a_ref, j_ref):
    n = R
    groups = n // 8
    j_ref[...] = identity(n)
    sub = lax.broadcasted_iota(jnp.int32, (8, n), 0)
    for p in range(groups):
        r0 = 8 * p
        panel = a_ref[r0 : r0 + 8, :]
        eye_p = j_ref[r0 : r0 + 8, :]
        cols = [jnp.broadcast_to(panel[:, r0 + c : r0 + c + 1], (8, n)) for c in range(8)]
        a = [[jnp.broadcast_to(cols[c][s : s + 1, :], (8, n)) for c in range(s + 1)] for s in range(8)]
        rs = [None] * 8
        low = [[None] * 8 for _ in range(8)]
        for r in range(8):
            rs[r] = lax.rsqrt(a[r][r])
            for s in range(r + 1, 8):
                low[s][r] = a[s][r] * rs[r]
            for s in range(r + 1, 8):
                for c in range(r + 1, s + 1):
                    a[s][c] = a[s][c] - low[s][r] * low[c][r]
        urow = []
        jrow = []
        for r in range(8):
            ur = jnp.broadcast_to(panel[r : r + 1, :], (8, n))
            jr = jnp.broadcast_to(eye_p[r : r + 1, :], (8, n))
            for k in range(r):
                ur = ur - low[r][k] * urow[k]
                jr = jr - low[r][k] * jrow[k]
            urow.append(ur * rs[r])
            jrow.append(jr * rs[r])
        done = jrow[0]
        for r in range(1, 8):
            done = jnp.where(sub == r, jrow[r], done)
        j_ref[r0 : r0 + 8, :] = done
        for g in range(p + 1, groups):
            ag = a_ref[8 * g : 8 * g + 8, :]
            jg = j_ref[8 * g : 8 * g + 8, :]
            acc_a, acc_j = ag, jg
            m = []
            for r in range(8):
                b = jnp.broadcast_to(ag[:, r0 + r : r0 + r + 1], (8, n))
                for k in range(r):
                    b = b - low[r][k] * m[k]
                m.append(b * rs[r])
                acc_a = acc_a - m[r] * urow[r]
                acc_j = acc_j - m[r] * jrow[r]
            a_ref[8 * g : 8 * g + 8, :] = acc_a
            j_ref[8 * g : 8 * g + 8, :] = acc_j


def chunks(start, stop, size=256):
    return [(c, min(c + size, stop)) for c in range(start, stop, size)]


def blk(i):
    return slice(i * R, (i + 1) * R)


def leaf_kernel(
    count_ref, xr_ref, xc_ref, basis_ref, rhs_ref,
    row_ref, trail_ref, y_ref, u_ref, li_ref,
    a_ref, j_ref, right_ref, left_ref, yh_ref, yl_ref,
):
    slots, columns = y_ref.shape
    nb = slots // R
    levels = basis_ref.shape[1] // R
    count = count_ref[0]
    live_lane = (lax.broadcasted_iota(jnp.int32, (1, slots), 1) < count).astype(F32)
    live_sub = (lax.broadcasted_iota(jnp.int32, (slots, 1), 0) < count).astype(F32)
    for b in range(nb):
        live_b = live_sub[blk(b), :]
        y_ref[blk(b), : levels * R] = basis_ref[blk(b), :] * live_b
        y_ref[blk(b), levels * R :] = rhs_ref[blk(b), :] * live_b
        for c0, c1 in chunks(b * R, slots, 128):
            dist = None
            for d in range(3):
                diff = xc_ref[blk(b), d : d + 1] - xr_ref[d : d + 1, c0:c1]
                dist = diff * diff if dist is None else dist + diff * diff
            kern = jnp.exp(-GAMMA_RATE * dist) * live_b * live_lane[:, c0:c1]
            if c0 == b * R:
                kern = kern + NUGGET_VALUE * identity(R)
            u_ref[blk(b), c0:c1] = kern

    def step(b, carry):
        here = pl.ds(pl.multiple_of(b * R, R), R)
        a_ref[...] = u_ref[here, here]
        factor(a_ref, j_ref)
        li_ref[here, :] = j_ref[...]
        for static_b in range(nb):

            @pl.when(b == static_b)
            def _(b=static_b):
                inv = wide(j_ref[...])
                for c0, c1 in chunks((b + 1) * R, slots, 256):
                    new = dot(inv, tall(u_ref[blk(b), c0:c1]))
                    u_ref[blk(b), c0:c1] = new
                    right_ref[:, c0:c1] = tall(new)
                    for e0, e1 in chunks(c0, c1, R):
                        left_ref[e0:e1, :] = wide(new[:, e0 - c0 : e1 - c0].T)
                for c0, c1 in chunks(0, columns, 256):
                    new = dot(inv, tall(y_ref[blk(b), c0:c1]))
                    y_ref[blk(b), c0:c1] = new
                    stacked = tall(new)
                    right_ref[:, slots + c0 : slots + c1] = stacked
                    yh_ref[blk(b), c0:c1] = stacked[:R]
                    yl_ref[blk(b), c0:c1] = stacked[R : 2 * R]
                for i in range(b + 1, nb):
                    left = left_ref[blk(i), :]
                    for c0, c1 in chunks(i * R, slots, 256):
                        u_ref[blk(i), c0:c1] = u_ref[blk(i), c0:c1] - dot(left, right_ref[:, c0:c1])
                    for c0, c1 in chunks(0, columns, 256):
                        y_ref[blk(i), c0:c1] = y_ref[blk(i), c0:c1] - dot(
                            left, right_ref[:, slots + c0 : slots + c1]
                        )

        return carry

    lax.fori_loop(0, nb, step, 0)
    offset = 0
    for k in range(levels):
        high, low = split(y_ref[:, blk(k)].T)
        target = row_ref if k == 0 else trail_ref
        base = 0 if k == 0 else offset
        for c0, c1 in chunks(k * R, columns, 256):
            yh = yh_ref[:, c0:c1]
            value = dot(high, yh) + dot(high, yl_ref[:, c0:c1]) + dot(low, yh)
            target[:, base + c0 - k * R : base + c1 - k * R] = value
        if k > 0:
            offset += columns - k * R


def level_kernel(own_ref, sib_ref, e_ref, side_ref, z_ref, w_ref, q_ref, a_ref, j_ref):
    width = own_ref.shape[1]
    side = side_ref[0]
    mine = pl.ds(pl.multiple_of(side * R, R), R)
    other = pl.ds(pl.multiple_of((1 - side) * R, R), R)
    q_ref[mine, :] = own_ref[...]
    q_ref[other, :] = sib_ref[...]
    e_stack = tall(e_ref[...])
    up = e_ref[:R, :].T
    low = e_ref[R:, :].T
    first = dot3(up, q_ref[:R, :R])
    second = dot3(low, q_ref[R:, :R])
    h = dot(wide(jnp.concatenate([first, second], axis=1)), e_stack)
    both = wide(jnp.concatenate([up, low], axis=1))
    forcing = dot(both, tall(q_ref[:, R:]))
    h12 = 0.5 * (h[:R, R:] + h[R:, :R].T)
    h11 = h[:R, :R]
    h22 = h[R:, R:]
    a_ref[...] = 0.5 * (h11 + h11.T) + identity(R)
    factor(a_ref, j_ref)
    inv1 = j_ref[...]
    inv1w = wide(inv1)
    u12 = dot(inv1w, tall(h12))
    u12t = u12.T
    a_ref[...] = 0.5 * (h22 + h22.T) + identity(R) - dot3(u12t, u12)
    z1 = dot(inv1w, tall(forcing[:R]))
    z_ref[:R, :] = z1
    rest = forcing[R:] - dot3(u12t, z1)
    factor(a_ref, j_ref)
    inv2 = j_ref[...]
    z_ref[R:, :] = dot3(inv2, rest)
    e_own = e_ref[mine, :]
    w1 = dot3(e_own[:, :R], inv1.T)
    w2 = dot3(e_own[:, R:] - dot3(w1, u12), inv2.T)
    w_ref[:, :R] = w1
    w_ref[:, R:] = w2


def next_row_kernel(own_ref, sib_ref, z_ref, row_ref):
    width = row_ref.shape[1]
    row_ref[...] = own_ref[:, :width] + sib_ref[:, :width] - dot3(z_ref[:, :R].T, z_ref[...])


def rest_kernel(own_ref, sib_ref, z_ref, w_ref, trail_ref, g_ref):
    width = z_ref.shape[1]
    source, target = width, 0
    for k in range(1, width // R - 1):
        size = width - k * R
        trail_ref[:, target : target + size] = (
            own_ref[:, source : source + size]
            + sib_ref[:, source : source + size]
            - dot3(z_ref[:, blk(k)].T, z_ref[:, k * R :])
        )
        source += size
        target += size
    g_ref[...] = dot3(w_ref[...], z_ref[...])


def g_kernel(z_ref, w_ref, g_ref):
    g_ref[...] = dot3(w_ref[...], z_ref[...])


def final_kernel(*refs):
    y_ref, u_ref, li_ref = refs[:3]
    levels = len(refs) - 6
    g_refs = refs[3 : 3 + levels]
    out_ref, v_ref, x_ref = refs[3 + levels :]
    slots = y_ref.shape[0]
    nb = slots // R
    for k in reversed(range(levels)):
        g = g_refs[k]
        value = -g[:, g.shape[1] - R :]
        if k < levels - 1:
            value = value - dot3(g[:, : g.shape[1] - R], v_ref[(k + 1) * R :, :])
        v_ref[blk(k), :] = value
    vt = tall(v_ref[...])
    for b in range(nb):
        x_ref[blk(b), :] = y_ref[blk(b), levels * R :] + dot(wide(y_ref[blk(b), : levels * R]), vt)
    for b in reversed(range(nb)):
        value = dot3(li_ref[blk(b), :].T, x_ref[blk(b), :])
        out_ref[blk(b), :] = value
        if b > 0:
            x_ref[: b * R, :] = x_ref[: b * R, :] - dot3(u_ref[: b * R, blk(b)], value)


def f32(*shape):
    return jax.ShapeDtypeStruct(shape, F32)


def call(kernel, outs, ins, scratch=(), **kw):
    return pl.pallas_call(
        kernel,
        out_shape=outs,
        in_specs=ins,
        out_specs=jax.tree.map(lambda _: VMEM, outs),
        scratch_shapes=list(scratch),
        compiler_params=PARAMS,
        **kw,
    )


def shards(points, order, counts, basis, right_side, coupling):
    slots = points.shape[1]
    levels = basis.shape[1] // R
    columns = levels * R + right_side.shape[1]
    ordered = points[:, order[0]]
    trail_width = sum(columns - k * R for k in range(1, levels))
    row, trail, y, u, li = call(
        leaf_kernel,
        (f32(R, columns), f32(R, trail_width), f32(slots, columns), f32(slots, slots), f32(slots, R)),
        [SMEM, VMEM, VMEM, VMEM, VMEM],
        [
            pltpu.VMEM((R, R), F32),
            pltpu.VMEM((R, R), F32),
            pltpu.VMEM((3 * R, slots + columns), BF16),
            pltpu.VMEM((slots, 3 * R), BF16),
            pltpu.VMEM((slots, columns), BF16),
            pltpu.VMEM((slots, columns), BF16),
        ],
    )(counts, ordered, ordered.T, basis, right_side)
    subs = lax.axis_size("sub")
    sub_bits = subs.bit_length() - 1
    position = lax.axis_index("leaf") * subs + lax.axis_index("sub")
    neighbour = {0: ("sub", 1), 1: ("sub", 3), 2: ("leaf", 1), 3: ("leaf", 2), 4: ("leaf", 6), 5: ("leaf", 8), 6: ("leaf", 24)}

    def swap(x, level):
        axis, mask = neighbour[level]
        return lax.ppermute(x, axis, [(i, i ^ mask) for i in range(lax.axis_size(axis))])

    gs = []
    for level in range(levels):
        last = level == levels - 1
        width = columns - (level + 1) * R
        sib = swap(row, level)
        if not last:
            sib_trail = swap(trail, level)
        side = (position >> level & 1).reshape(1)
        z, w = call(
            level_kernel,
            (f32(2 * R, width), f32(R, 2 * R)),
            [VMEM, VMEM, VMEM, SMEM],
            [pltpu.VMEM((2 * R, width + R), F32), pltpu.VMEM((R, R), F32), pltpu.VMEM((R, R), F32)],
            cost_estimate=pl.CostEstimate(flops=20_000_000_000, bytes_accessed=4_000_000, transcendentals=0),
        )(row, sib, coupling[level], side)
        if last:
            gs.append(call(g_kernel, f32(R, width), [VMEM, VMEM])(z, w))
        else:
            row = call(next_row_kernel, f32(R, width), [VMEM] * 3)(trail, sib_trail, z)
            if level < levels - 2:
                trail, g = call(rest_kernel, (f32(R, trail.shape[1] - width), f32(R, width)), [VMEM] * 4)(
                    trail, sib_trail, z, w
                )
            else:
                g = call(g_kernel, f32(R, width), [VMEM, VMEM])(z, w)
            gs.append(g)
    return call(
        final_kernel,
        f32(slots, columns - levels * R),
        [VMEM] * (3 + levels),
        [pltpu.VMEM((levels * R, R), F32), pltpu.VMEM((slots, R), F32)],
    )(y, u, li, *gs)


def solution(mesh):
    placed = (
        P(None, ("leaf", "sub")),
        P(("leaf", "sub"), None),
        P(("leaf", "sub")),
        P(("leaf", "sub"), None),
        P(("leaf", "sub"), None),
        P(),
    )
    return jax.shard_map(
        shards, mesh=mesh, in_specs=placed, out_specs=P(("leaf", "sub"), None), check_vma=False
    )
```

time: 1220 us -> 291 us (0.24)
  other arithmetic: 687 us -> 0.7 us
  matrix products: 190 us -> 0 us
  Pallas kernels: 0 us -> 184 us
  local copies, waits for them, and re-layouts: 119 us -> 17.8 us
  waiting for transfers between devices: 141 us -> 66 us
  starting transfers between devices: 57.8 us -> 18.4 us
  between operations: 17.2 us -> 1 us
    another operation x97 -> x0, other arithmetic: 657 us -> none  [the longest x49 255 us: couple(): lower_tri = jnp.linalg.cholesky(coupled)]
    pallas_call x0 -> x22, Pallas kernels: none -> 184 us  [the longest x7 84.3 us: shards(): call(level_kernel, (f32(2 * R, width), f32(R, 2 * R)), [VMEM, VMEM, VMEM,...]
    another operation x100 -> x0, matrix products: 113 us -> none  [the longest x30 49.1 us: leaf_solve(): solved = jax.scipy.linalg.cho_solve((lower_tri, True), stacked)]
    dot_general x63 -> x0, matrix products: 76.9 us -> none  [the longest x7 28.1 us: shards(): jnp.dot(solved[:, col_start:col_start + R], own_mixed, precision=highest)]
    ppermute x28 -> x13, waiting for transfers between devices: 141 us -> 66 us  [swap(): lax.ppermute(x, axis, [(i, i ^ mask) for i in range(lax.axis_size(axis))])]
    another operation x95 -> x0, local copies, waits for them, and re-layouts: 62.9 us -> none
    ppermute x28 -> x13, starting transfers between devices: 57.8 us -> 18.4 us  [swap(): lax.ppermute(x, axis, [(i, i ^ mask) for i in range(lax.axis_size(axis))])]
    dot_general x14 -> x0, local copies, waits for them, and re-layouts: 14.2 us -> none  [the longest x7 7.77 us: couple(): jnp.dot(lower_half.T, jnp.dot(second_block, lower_half, precision=highest...]
  transfers between devices with their start and end apart: 28 -> 13, of which waited for: 28 -> 8; matrix products, arithmetic and copies ran while one was open for 0% -> 1% of each run, Pallas kernels for 0% -> 32%
where the time goes in v1:
time: 291 us; the launch traced here: 288 us
  Pallas kernels  184 us (63%)
  waiting for transfers between devices  66 us (23%)
  starting transfers between devices  18.4 us (6%)
  local copies, waits for them, and re-layouts  17.8 us (6%)
    pallas_call x7, Pallas kernels, shards(): call(level_kernel, (f32(2 * R, width), f32(R, 2 * R)), [VMEM, VMEM, VMEM,...  84.3 us
    ppermute x13, waiting for transfers between devices, swap(): lax.ppermute(x, axis, [(i, i ^ mask) for i in range(lax.axis_size(axis))])  66 us
    pallas_call x1, Pallas kernels, shards(): call(leaf_kernel, (f32(R, columns), f32(R, trail_width), f32(slots, colum...  53 us
    ppermute x13, starting transfers between devices, swap(): lax.ppermute(x, axis, [(i, i ^ mask) for i in range(lax.axis_size(axis))])  18.4 us
    pallas_call x5, Pallas kernels, shards(): call(rest_kernel, (f32(R, trail.shape[1] - width), f32(R, width)), [VMEM]...  16.5 us
    pallas_call x6, Pallas kernels, shards(): row = call(next_row_kernel, f32(R, width), [VMEM] * 3)(trail, sib_trail, z)  15.9 us
    unnamed x29, local copies, waits for them, and re-layouts  11.5 us
    pallas_call x1, Pallas kernels, shards(): call(final_kernel, f32(slots, columns - levels * R), [VMEM] * (3 + levels...  11.1 us
  transfers between devices with their start and end apart: 13, of which 8 were waited for; matrix products, arithmetic and copies ran while one was open for 1% of the time, Pallas kernels for 32%

profile of v1, /device:TPU:0, one launch (start us, length us, event | category | flops | bytes accessed | tf_op | source)
XLA Modules:
  0.0 288.4 jit_solution(12594446877638046022)
XLA Ops:
  1.4 0.9 copy.9
  2.3 2.8 gather_fusion
  5.1 0.8 copy.10
  5.9 53.0 %shard_map.64 = (f32[128,1024]{1,0:T(8,128)}, f32[128,3456]{1,0:T(8,128)}, f32[1024,1024]{1,0:T(8,128)}, f32[1024,1024]{1,0:T(8,128)}, f32[1024,128]{1,0:T(8,128)}) custom-call(s32[1]{0:T(128)S(6)} %copy.11.count_ref, f32[3,1024]{1,0:T(4,128)} %bitcast.25, f32[1024,3]{1,0:T(8,128)} %copy-done.4, f32[1024,896]{1,0:T(8,128)} %basis_ref.1, f32[1024,128]{1,0:T(8,128)} %rhs_ref.1), custom_call_target="tpu_custom_call" | custom-call | tf_op jit(solution)/shard_map/pallas_call | solution.py:288
  58.9 1.6 collective-permute-start.1
  60.9 2.6 slice_bitcast_fusion
  63.6 10.4 %collective-permute-done.1.sib_ref = f32[128,1024]{1,0:T(8,128)S(1)} collective-permute-done((f32[128,1024]{1,0:T(8,128)}, f32[128,1024]{1,0:T(8,128)S(1)}, u32[]{:S(2)}, u32[]{:S(2)}) %collective-permute-start.1) | collective-permute-done | bytes 524320 | tf_op jit(solution)/shard_map/ppermute | solution.py:308
  74.0 0.8 copy-done.7
  74.7 12.4 %shard_map.65 = (f32[256,896]{1,0:T(8,128)}, f32[128,256]{1,0:T(8,128)}) custom-call(f32[128,1024]{1,0:T(8,128)} %get-tuple-element.38.own_ref, f32[128,1024]{1,0:T(8,128)} %copy-done.7, f32[256,256]{1,0:T(8,128)} %get-tuple-element.68.e_ref, s32[1]{0:T(128)} %bitcast.4.side_ref), custom_call_target="tpu_custom_call" | custom-call | flops 20000000000 | bytes 4000000 | tf_op jit(solution)/shard_map/pallas_call | solution.py:318
  87.2 23.3 %collective-permute-done.sib_ref = f32[128,3456]{1,0:T(8,128)S(1)} collective-permute-done((f32[128,3456]{1,0:T(8,128)}, f32[128,3456]{1,0:T(8,128)S(1)}, u32[]{:S(2)}, u32[]{:S(2)}) %collective-permute-start) | collective-permute-done | bytes 1769504 | tf_op jit(solution)/shard_map/ppermute | solution.py:308
  110.5 1.2 copy-done
  111.7 3.5 %shard_map.67.own_ref = f32[128,896]{1,0:T(8,128)} custom-call(f32[128,3456]{1,0:T(8,128)} %get-tuple-element.37.own_ref, f32[128,3456]{1,0:T(8,128)} %copy-done, f32[256,896]{1,0:T(8,128)} %get-tuple-element.39.z_ref), custom_call_target="tpu_custom_call" | custom-call | tf_op jit(solution)/shard_map/pallas_call | solution.py:328
  115.2 3.0 %collective-permute-start.3 = (f32[128,896]{1,0:T(8,128)}, f32[128,896]{1,0:T(8,128)S(1)}, u32[]{:S(2)}, u32[]{:S(2)}) collective-permute-start(f32[128,896]{1,0:T(8,128)} %shard_map.67.own_ref), channel_id=1, source_target_pairs={{0,3},{1,2},{2,1},{3,0},{4,7},{5,6},{6,5},{7,4},{8,11},{9,10},{10,... | collective-permute-start | bytes 1376264 | tf_op jit(solution)/shard_map/ppermute | solution.py:308
  118.2 4.6 %shard_map.66 = (f32[128,2560]{1,0:T(8,128)}, f32[128,896]{1,0:T(8,128)}) custom-call(f32[128,3456]{1,0:T(8,128)} %get-tuple-element.37.own_ref, f32[128,3456]{1,0:T(8,128)} %copy-done, f32[256,896]{1,0:T(8,128)} %get-tuple-element.39.z_ref, f32[128,256]{1,0:T(8,128)} %get-tuple-element.40.w_ref), custom_call_target="tpu_custom_call" | custom-call | tf_op jit(solution)/shard_map/pallas_call | solution.py:330
  123.2 6.9 %collective-permute-done.3.sib_ref = f32[128,896]{1,0:T(8,128)S(1)} collective-permute-done((f32[128,896]{1,0:T(8,128)}, f32[128,896]{1,0:T(8,128)S(1)}, u32[]{:S(2)}, u32[]{:S(2)}) %collective-permute-start.3) | collective-permute-done | bytes 458784 | tf_op jit(solution)/shard_map/ppermute | solution.py:308
  130.1 0.8 copy-done.8
  130.8 12.2 %shard_map.68 = (f32[256,768]{1,0:T(8,128)}, f32[128,256]{1,0:T(8,128)}) custom-call(f32[128,896]{1,0:T(8,128)} %shard_map.67.own_ref, f32[128,896]{1,0:T(8,128)} %copy-done.8, f32[256,256]{1,0:T(8,128)} %get-tuple-element.67.e_ref, s32[1]{0:T(128)} %bitcast.6.side_ref), custom_call_target="tpu_custom_call" | custom-call | flops 20000000000 | bytes 4000000 | tf_op jit(solution)/shard_map/pallas_call | solution.py:318
  143.0 13.1 %collective-permute-done.2.sib_ref = f32[128,2560]{1,0:T(8,128)S(1)} collective-permute-done((f32[128,2560]{1,0:T(8,128)}, f32[128,2560]{1,0:T(8,128)S(1)}, u32[]{:S(2)}, u32[]{:S(2)}) %collective-permute-start.2) | collective-permute-done | bytes 1310752 | tf_op jit(solution)/shard_map/ppermute | solution.py:308
  156.1 1.1 copy-done.1
  157.2 3.0 %shard_map.70.own_ref = f32[128,768]{1,0:T(8,128)} custom-call(f32[128,2560]{1,0:T(8,128)} %get-tuple-element.42.own_ref, f32[128,2560]{1,0:T(8,128)} %copy-done.1, f32[256,768]{1,0:T(8,128)} %get-tuple-element.43.z_ref), custom_call_target="tpu_custom_call" | custom-call | tf_op jit(solution)/shard_map/pallas_call | solution.py:328
  160.2 3.8 %shard_map.69 = (f32[128,1792]{1,0:T(8,128)}, f32[128,768]{1,0:T(8,128)}) custom-call(f32[128,2560]{1,0:T(8,128)} %get-tuple-element.42.own_ref, f32[128,2560]{1,0:T(8,128)} %copy-done.1, f32[256,768]{1,0:T(8,128)} %get-tuple-element.43.z_ref, f32[128,256]{1,0:T(8,128)} %get-tuple-element.44.w_ref), custom_call_target="tpu_custom_call" | custom-call | tf_op jit(solution)/shard_map/pallas_call | solution.py:330
  164.8 0.8 copy-done.9
  165.5 12.1 %shard_map.71 = (f32[256,640]{1,0:T(8,128)}, f32[128,256]{1,0:T(8,128)}) custom-call(f32[128,768]{1,0:T(8,128)} %shard_map.70.own_ref, f32[128,768]{1,0:T(8,128)} %copy-done.9, f32[256,256]{1,0:T(8,128)} %get-tuple-element.66.e_ref, s32[1]{0:T(128)} %bitcast.8.side_ref), custom_call_target="tpu_custom_call" | custom-call | flops 20000000000 | bytes 4000000 | tf_op jit(solution)/shard_map/pallas_call | solution.py:318
  177.6 1.0 copy-done.2
  178.6 2.8 shard_map.73.own_ref
  181.4 2.1 collective-permute-start.7
  183.5 3.2 %shard_map.72 = (f32[128,1152]{1,0:T(8,128)}, f32[128,640]{1,0:T(8,128)}) custom-call(f32[128,1792]{1,0:T(8,128)} %get-tuple-element.46.own_ref, f32[128,1792]{1,0:T(8,128)} %copy-done.2, f32[256,640]{1,0:T(8,128)} %get-tuple-element.47.z_ref, f32[128,256]{1,0:T(8,128)} %get-tuple-element.48.w_ref), custom_call_target="tpu_custom_call" | custom-call | tf_op jit(solution)/shard_map/pallas_call | solution.py:330
  187.1 5.1 %collective-permute-done.7.sib_ref = f32[128,640]{1,0:T(8,128)S(1)} collective-permute-done((f32[128,640]{1,0:T(8,128)}, f32[128,640]{1,0:T(8,128)S(1)}, u32[]{:S(2)}, u32[]{:S(2)}) %collective-permute-start.7) | collective-permute-done | bytes 327712 | tf_op jit(solution)/shard_map/ppermute | solution.py:308
  192.2 0.8 copy-done.10
  193.0 12.2 %shard_map.74 = (f32[256,512]{1,0:T(8,128)}, f32[128,256]{1,0:T(8,128)}) custom-call(f32[128,640]{1,0:T(8,128)} %shard_map.73.own_ref, f32[128,640]{1,0:T(8,128)} %copy-done.10, f32[256,256]{1,0:T(8,128)} %get-tuple-element.65.e_ref, s32[1]{0:T(128)} %bitcast.10.side_ref), custom_call_target="tpu_custom_call" | custom-call | flops 20000000000 | bytes 4000000 | tf_op jit(solution)/shard_map/pallas_call | solution.py:318
  205.2 0.9 copy-done.3
  206.1 2.4 shard_map.76.own_ref
  208.5 4.2 %collective-permute-start.9 = (f32[128,512]{1,0:T(8,128)}, f32[128,512]{1,0:T(8,128)S(1)}, u32[]{:S(2)}, u32[]{:S(2)}) collective-permute-start(f32[128,512]{1,0:T(8,128)} %shard_map.76.own_ref), channel_id=1, source_target_pairs={{0,24},{4,28},{8,16},{12,20},{16,8},{20,12},{24,0},{28,4},{32,56},... | collective-permute-start | bytes 786440 | tf_op jit(solution)/shard_map/ppermute | solution.py:308
  212.7 2.6 shard_map.75
  215.5 4.3 %collective-permute-done.9.sib_ref = f32[128,512]{1,0:T(8,128)S(1)} collective-permute-done((f32[128,512]{1,0:T(8,128)}, f32[128,512]{1,0:T(8,128)S(1)}, u32[]{:S(2)}, u32[]{:S(2)}) %collective-permute-start.9) | collective-permute-done | bytes 262176 | tf_op jit(solution)/shard_map/ppermute | solution.py:308
  220.5 11.9 %shard_map.77 = (f32[256,384]{1,0:T(8,128)}, f32[128,256]{1,0:T(8,128)}) custom-call(f32[128,512]{1,0:T(8,128)} %shard_map.76.own_ref, f32[128,512]{1,0:T(8,128)} %copy-done.11, f32[256,256]{1,0:T(8,128)} %get-tuple-element.64.e_ref, s32[1]{0:T(128)} %bitcast.12.side_ref), custom_call_target="tpu_custom_call" | custom-call | flops 20000000000 | bytes 4000000 | tf_op jit(solution)/shard_map/pallas_call | solution.py:318
  233.1 2.2 shard_map.79.own_ref
  235.4 1.6 collective-permute-start.10
  236.9 2.2 shard_map.78
  239.8 1.4 collective-permute-done.10.sib_ref
  241.9 11.6 %shard_map.80 = (f32[256,256]{1,0:T(8,128)}, f32[128,256]{1,0:T(8,128)}) custom-call(f32[128,384]{1,0:T(8,128)} %shard_map.79.own_ref, f32[128,384]{1,0:T(8,128)} %copy-done.12, f32[256,256]{1,0:T(8,128)} %get-tuple-element.69.e_ref, s32[1]{0:T(128)} %bitcast.14.side_ref), custom_call_target="tpu_custom_call" | custom-call | flops 20000000000 | bytes 4000000 | tf_op jit(solution)/shard_map/pallas_call | solution.py:318
  254.2 2.0 shard_map.82.own_ref
  256.2 3.2 %collective-permute-start.12 = (f32[128,256]{1,0:T(8,128)}, f32[128,256]{1,0:T(8,128)S(1)}, u32[]{:S(2)}, u32[]{:S(2)}) collective-permute-start(f32[128,256]{1,0:T(8,128)} %shard_map.82.own_ref), channel_id=1, source_target_pairs={{0,96},{4,100},{8,104},{12,108},{16,112},{20,116},{24,120},{28,124... | collective-permute-start | bytes 393224 | tf_op jit(solution)/shard_map/ppermute | solution.py:308
  259.4 1.9 shard_map.81.refs_8_
  261.3 1.5 collective-permute-done.12.sib_ref
  263.5 11.8 %shard_map.83 = (f32[256,128]{1,0:T(8,128)}, f32[128,256]{1,0:T(8,128)}) custom-call(f32[128,256]{1,0:T(8,128)} %shard_map.82.own_ref, f32[128,256]{1,0:T(8,128)} %copy-done.13, f32[256,256]{1,0:T(8,128)} %get-tuple-element.63.e_ref, s32[1]{0:T(128)} %bitcast.16.side_ref), custom_call_target="tpu_custom_call" | custom-call | flops 20000000000 | bytes 4000000 | tf_op jit(solution)/shard_map/pallas_call | solution.py:318
  275.2 1.8 shard_map.84.refs_9_
  277.0 11.1 %shard_map.85 = f32[1024,128]{1,0:T(8,128)} custom-call(f32[1024,1024]{1,0:T(8,128)} %get-tuple-element.34.refs_0_, f32[1024,1024]{1,0:T(8,128)} %get-tuple-element.35.refs_1_, f32[1024,128]{1,0:T(8,128)} %get-tuple-element.36.refs_2_, f32[128,896]{1,0:T(8,128)} %get-tuple-element.41.refs_3_, f32[128,768]{1,0:T(8,128)} %get-tuple-element.45.refs_4_, ...), custom_call_target="tpu_custom_call" | custom-call | tf_op jit(solution)/shard_map/pallas_call | solution.py:336
  (34 shorter events, 6.9 us)
Async XLA Ops:
  5.1 0.8 copy-start.4
  58.9 15.1 %collective-permute-start.1 = (f32[128,1024]{1,0:T(8,128)}, f32[128,1024]{1,0:T(8,128)S(1)}, u32[]{:S(2)}, u32[]{:S(2)}) collective-permute-start(f32[128,1024]{1,0:T(8,128)} %get-tuple-element.38.own_ref), channel_id=1, source_target_pairs={{0,1},{1,0},{2,3},{3,2},{4,5},{5,4},{6,7},{7,6},{8,9},{9,8},{10,11... | collective-permute-start | bytes 1572872 | tf_op jit(solution)/shard_map/ppermute | solution.py:308
  60.5 50.1 %collective-permute-start = (f32[128,3456]{1,0:T(8,128)}, f32[128,3456]{1,0:T(8,128)S(1)}, u32[]{:S(2)}, u32[]{:S(2)}) collective-permute-start(f32[128,3456]{1,0:T(8,128)} %get-tuple-element.37.own_ref), channel_id=1, source_target_pairs={{0,1},{1,0},{2,3},{3,2},{4,5},{5,4},{6,7},{7,6},{8,9},{9,8},{10,11... | collective-permute-start | bytes 5308424 | tf_op jit(solution)/shard_map/ppermute | solution.py:308
  74.0 0.8 copy-start.7
  110.5 1.2 copy-start
  115.2 14.9 %collective-permute-start.3 = (f32[128,896]{1,0:T(8,128)}, f32[128,896]{1,0:T(8,128)S(1)}, u32[]{:S(2)}, u32[]{:S(2)}) collective-permute-start(f32[128,896]{1,0:T(8,128)} %shard_map.67.own_ref), channel_id=1, source_target_pairs={{0,3},{1,2},{2,1},{3,0},{4,7},{5,6},{6,5},{7,4},{8,11},{9,10},{10,... | collective-permute-start | bytes 1376264 | tf_op jit(solution)/shard_map/ppermute | solution.py:308
  122.8 33.3 %collective-permute-start.2 = (f32[128,2560]{1,0:T(8,128)}, f32[128,2560]{1,0:T(8,128)S(1)}, u32[]{:S(2)}, u32[]{:S(2)}) collective-permute-start(f32[128,2560]{1,0:T(8,128)} %get-tuple-element.42.own_ref), channel_id=1, source_target_pairs={{0,3},{1,2},{2,1},{3,0},{4,7},{5,6},{6,5},{7,4},{8,11},{9,10},{10,... | collective-permute-start | bytes 3932168 | tf_op jit(solution)/shard_map/ppermute | solution.py:308
  130.1 0.8 copy-start.8
  156.1 1.1 copy-start.1
  160.2 4.5 %collective-permute-start.5 = (f32[128,768]{1,0:T(8,128)}, f32[128,768]{1,0:T(8,128)S(1)}, u32[]{:S(2)}, u32[]{:S(2)}) collective-permute-start(f32[128,768]{1,0:T(8,128)} %shard_map.70.own_ref), channel_id=1, source_target_pairs={{0,4},{4,0},{8,12},{12,8},{16,20},{20,16},{24,28},{28,24},{32,36},... | collective-permute-start | bytes 1179656 | tf_op jit(solution)/shard_map/ppermute | solution.py:308
  164.1 13.6 %collective-permute-start.4 = (f32[128,1792]{1,0:T(8,128)}, f32[128,1792]{1,0:T(8,128)S(1)}, u32[]{:S(2)}, u32[]{:S(2)}) collective-permute-start(f32[128,1792]{1,0:T(8,128)} %get-tuple-element.46.own_ref), channel_id=1, source_target_pairs={{0,4},{4,0},{8,12},{12,8},{16,20},{20,16},{24,28},{28,24},{32,36},... | collective-permute-start | bytes 2752520 | tf_op jit(solution)/shard_map/ppermute | solution.py:308
  164.8 0.8 copy-start.9
  177.6 1.0 copy-start.2
  181.4 10.9 %collective-permute-start.7 = (f32[128,640]{1,0:T(8,128)}, f32[128,640]{1,0:T(8,128)S(1)}, u32[]{:S(2)}, u32[]{:S(2)}) collective-permute-start(f32[128,640]{1,0:T(8,128)} %shard_map.73.own_ref), channel_id=1, source_target_pairs={{0,8},{4,12},{8,0},{12,4},{16,24},{20,28},{24,16},{28,20},{32,40},... | collective-permute-start | bytes 983048 | tf_op jit(solution)/shard_map/ppermute | solution.py:308
  186.7 18.5 %collective-permute-start.6 = (f32[128,1152]{1,0:T(8,128)}, f32[128,1152]{1,0:T(8,128)S(1)}, u32[]{:S(2)}, u32[]{:S(2)}) collective-permute-start(f32[128,1152]{1,0:T(8,128)} %get-tuple-element.50.own_ref), channel_id=1, source_target_pairs={{0,8},{4,12},{8,0},{12,4},{16,24},{20,28},{24,16},{28,20},{32,40},... | collective-permute-start | bytes 1769480 | tf_op jit(solution)/shard_map/ppermute | solution.py:308
  192.2 0.8 copy-start.10
  205.2 0.9 copy-start.3
  208.5 11.3 %collective-permute-start.9 = (f32[128,512]{1,0:T(8,128)}, f32[128,512]{1,0:T(8,128)S(1)}, u32[]{:S(2)}, u32[]{:S(2)}) collective-permute-start(f32[128,512]{1,0:T(8,128)} %shard_map.76.own_ref), channel_id=1, source_target_pairs={{0,24},{4,28},{8,16},{12,20},{16,8},{20,12},{24,0},{28,4},{32,56},... | collective-permute-start | bytes 786440 | tf_op jit(solution)/shard_map/ppermute | solution.py:308
  215.4 17.1 %collective-permute-start.8 = (f32[128,640]{1,0:T(8,128)}, f32[128,640]{1,0:T(8,128)S(1)}, u32[]{:S(2)}, u32[]{:S(2)}) collective-permute-start(f32[128,640]{1,0:T(8,128)} %get-tuple-element.54.own_ref), channel_id=1, source_target_pairs={{0,24},{4,28},{8,16},{12,20},{16,8},{20,12},{24,0},{28,4},{32,56},... | collective-permute-start | bytes 983048 | tf_op jit(solution)/shard_map/ppermute | solution.py:308
  219.8 0.7 copy-start.11
  232.4 0.7 copy-start.5
  235.4 5.9 %collective-permute-start.10 = (f32[128,384]{1,0:T(8,128)}, f32[128,384]{1,0:T(8,128)S(1)}, u32[]{:S(2)}, u32[]{:S(2)}) collective-permute-start(f32[128,384]{1,0:T(8,128)} %shard_map.79.own_ref), channel_id=1, source_target_pairs={{0,32},{4,36},{8,40},{12,44},{16,48},{20,52},{24,56},{28,60},{32,0... | collective-permute-start | bytes 589832 | tf_op jit(solution)/shard_map/ppermute | solution.py:308
  239.2 14.4 %collective-permute-start.11 = (f32[128,256]{1,0:T(8,128)}, f32[128,256]{1,0:T(8,128)S(1)}, u32[]{:S(2)}, u32[]{:S(2)}) collective-permute-start(f32[128,256]{1,0:T(8,128)} %get-tuple-element.60.own_ref), channel_id=1, source_target_pairs={{0,32},{4,36},{8,40},{12,44},{16,48},{20,52},{24,56},{28,60},{32,0... | collective-permute-start | bytes 393224 | tf_op jit(solution)/shard_map/ppermute | solution.py:308
  241.3 0.7 copy-start.12
  253.5 0.7 copy-start.6
  256.2 6.6 %collective-permute-start.12 = (f32[128,256]{1,0:T(8,128)}, f32[128,256]{1,0:T(8,128)S(1)}, u32[]{:S(2)}, u32[]{:S(2)}) collective-permute-start(f32[128,256]{1,0:T(8,128)} %shard_map.82.own_ref), channel_id=1, source_target_pairs={{0,96},{4,100},{8,104},{12,108},{16,112},{20,116},{24,120},{28,124... | collective-permute-start | bytes 393224 | tf_op jit(solution)/shard_map/ppermute | solution.py:308
  262.8 0.7 copy-start.13

commit v2 on v1

--- a/solution.py
+++ b/solution.py
@@ -107,7 +107,7 @@
 
 def leaf_kernel(
     count_ref, xr_ref, xc_ref, basis_ref, rhs_ref,
-    row_ref, trail_ref, y_ref, u_ref, li_ref,
+    t_ref, y_ref, u_ref, li_ref,
     a_ref, j_ref, right_ref, left_ref, yh_ref, yl_ref,
 ):
     slots, columns = y_ref.shape
@@ -168,90 +168,208 @@
     offset = 0
     for k in range(levels):
         high, low = split(y_ref[:, blk(k)].T)
-        target = row_ref if k == 0 else trail_ref
-        base = 0 if k == 0 else offset
         for c0, c1 in chunks(k * R, columns, 256):
             yh = yh_ref[:, c0:c1]
             value = dot(high, yh) + dot(high, yl_ref[:, c0:c1]) + dot(low, yh)
-            target[:, base + c0 - k * R : base + c1 - k * R] = value
-        if k > 0:
-            offset += columns - k * R
-
-
-def level_kernel(own_ref, sib_ref, e_ref, side_ref, z_ref, w_ref, q_ref, a_ref, j_ref):
-    width = own_ref.shape[1]
-    side = side_ref[0]
-    mine = pl.ds(pl.multiple_of(side * R, R), R)
-    other = pl.ds(pl.multiple_of((1 - side) * R, R), R)
-    q_ref[mine, :] = own_ref[...]
-    q_ref[other, :] = sib_ref[...]
-    e_stack = tall(e_ref[...])
-    up = e_ref[:R, :].T
-    low = e_ref[R:, :].T
-    first = dot3(up, q_ref[:R, :R])
-    second = dot3(low, q_ref[R:, :R])
-    h = dot(wide(jnp.concatenate([first, second], axis=1)), e_stack)
-    both = wide(jnp.concatenate([up, low], axis=1))
-    forcing = dot(both, tall(q_ref[:, R:]))
-    h12 = 0.5 * (h[:R, R:] + h[R:, :R].T)
-    h11 = h[:R, :R]
-    h22 = h[R:, R:]
-    a_ref[...] = 0.5 * (h11 + h11.T) + identity(R)
-    factor(a_ref, j_ref)
-    inv1 = j_ref[...]
-    inv1w = wide(inv1)
-    u12 = dot(inv1w, tall(h12))
-    u12t = u12.T
-    a_ref[...] = 0.5 * (h22 + h22.T) + identity(R) - dot3(u12t, u12)
-    z1 = dot(inv1w, tall(forcing[:R]))
-    z_ref[:R, :] = z1
-    rest = forcing[R:] - dot3(u12t, z1)
-    factor(a_ref, j_ref)
-    inv2 = j_ref[...]
-    z_ref[R:, :] = dot3(inv2, rest)
-    e_own = e_ref[mine, :]
-    w1 = dot3(e_own[:, :R], inv1.T)
-    w2 = dot3(e_own[:, R:] - dot3(w1, u12), inv2.T)
-    w_ref[:, :R] = w1
-    w_ref[:, R:] = w2
-
-
-def next_row_kernel(own_ref, sib_ref, z_ref, row_ref):
-    width = row_ref.shape[1]
-    row_ref[...] = own_ref[:, :width] + sib_ref[:, :width] - dot3(z_ref[:, :R].T, z_ref[...])
-
-
-def rest_kernel(own_ref, sib_ref, z_ref, w_ref, trail_ref, g_ref):
-    width = z_ref.shape[1]
-    source, target = width, 0
-    for k in range(1, width // R - 1):
-        size = width - k * R
-        trail_ref[:, target : target + size] = (
-            own_ref[:, source : source + size]
-            + sib_ref[:, source : source + size]
-            - dot3(z_ref[:, blk(k)].T, z_ref[:, k * R :])
+            t_ref[:, offset + c0 - k * R : offset + c1 - k * R] = value
+        offset += columns - k * R
+
+
+def width_of(level, row, levels):
+    return sum((levels + 1 - k) * R for k in range(level, row))
+
+
+def levels_kernel(
+    levels, t_ref, e_ref, g_ref,
+    own_ref, sib_ref, zt_ref, zl_ref, bd_ref, h_ref, f_ref, eb_ref, et_ref, u_ref, inv_ref, a_ref, j_ref,
+    send_sem, recv_sem,
+):
+    leaf, sub = lax.axis_index("leaf"), lax.axis_index("sub")
+    core, z, y = leaf % 2, (leaf // 2) % 4, leaf // 8
+    partner = [
+        (leaf, sub + 1 - 2 * (sub % 2)),
+        (leaf, 3 - sub),
+        (leaf + 1 - 2 * core, sub),
+        (y * 8 + (z + 1 - 2 * (z % 2)) * 2 + core, sub),
+        (y * 8 + (3 - z) * 2 + core, sub),
+        ((y + 1 - 2 * (y % 2)) * 8 + z * 2 + core, sub),
+        ((3 - y) * 8 + z * 2 + core, sub),
+    ]
+    position = leaf * 4 + sub
+    total = [width_of(k, levels, levels) for k in range(levels)]
+    own_base = [0] + [sum(total[1:k]) for k in range(1, levels)]
+    sib_base = [sum(total[:k]) for k in range(levels)]
+    z_base = [sum((levels - j) * R for j in range(k)) for k in range(levels)]
+    first_message = [sum(levels + 1 - j for j in range(k)) for k in range(levels)]
+
+    def span(level, part):
+        if part == 0:
+            return 0, R
+        start = R if part == 1 else width_of(level, level + part - 1, levels)
+        return start, width_of(level, level + part, levels) if part > 1 else width_of(level, level + 1, levels)
+
+    def own(level, c0, c1):
+        ref = t_ref if level == 0 else own_ref
+        return ref.at[:, own_base[level] + c0 : own_base[level] + c1]
+
+    def sib(level, c0, c1):
+        return sib_ref.at[:, sib_base[level] + c0 : sib_base[level] + c1]
+
+    def message(level, part):
+        c0, c1 = span(level, part)
+        index = first_message[level] + part
+        return pltpu.make_async_remote_copy(
+            src_ref=own(level, c0, c1),
+            dst_ref=sib(level, c0, c1),
+            send_sem=send_sem.at[index],
+            recv_sem=recv_sem.at[index],
+            device_id=partner[level],
+            device_id_type=pl.DeviceIdType.MESH,
         )
-        source += size
-        target += size
-    g_ref[...] = dot3(w_ref[...], z_ref[...])
-
-
-def g_kernel(z_ref, w_ref, g_ref):
-    g_ref[...] = dot3(w_ref[...], z_ref[...])
-
-
-def final_kernel(*refs):
-    y_ref, u_ref, li_ref = refs[:3]
-    levels = len(refs) - 6
-    g_refs = refs[3 : 3 + levels]
-    out_ref, v_ref, x_ref = refs[3 + levels :]
+
+    def side_slices(level):
+        side = (position // 2**level) % 2
+        mine = pl.ds(pl.multiple_of(side * R, R), R)
+        other = pl.ds(pl.multiple_of((1 - side) * R, R), R)
+        return mine, other
+
+    def prepare(level):
+        e = e_ref[level]
+        eb_ref[...] = wide(jnp.concatenate([e[:R].T, e[R:].T], axis=1))
+        et_ref[...] = tall(e)
+
+    def begin(level):
+        mine, other = side_slices(level)
+        bd_ref[mine, other] = jnp.zeros((R, R), F32)
+        bd_ref[other, mine] = jnp.zeros((R, R), F32)
+        bd_ref[mine, mine] = own(level, 0, R)[...]
+        message(level, 0).wait_recv()
+        bd_ref[other, other] = sib(level, 0, R)[...]
+        x = dot(eb_ref[...], tall(bd_ref[...]))
+        h = dot(wide(x), et_ref[...])
+        h = 0.5 * (h + h.T)
+        a_ref[...] = h[:R, :R] + identity(R)
+        h_ref[:R, :] = h[:R, R:]
+        h_ref[R:, :] = h[R:, R:]
+
+    def half(level):
+        mine, other = side_slices(level)
+        inverse = j_ref[...]
+        inv_ref[...] = inverse
+        stacked = wide(inverse)
+        upper = dot(stacked, tall(h_ref[:R, :]))
+        ut = upper.T
+        u_ref[...] = upper
+        left = wide(ut)
+        a_ref[...] = h_ref[R:, :] + identity(R) - dot(left, tall(upper))
+        message(level, 1).wait_recv()
+        w = (levels - level) * R
+        f_ref[mine, :w] = own(level, R, R + w)[...]
+        f_ref[other, :w] = sib(level, R, R + w)[...]
+        zb = z_base[level]
+        for c0, c1 in chunks(0, w):
+            forcing = dot(eb_ref[...], tall(f_ref[:, c0:c1]))
+            z1 = dot(stacked, tall(forcing[:R]))
+            f_ref[:R, c0:c1] = z1
+            f_ref[R:, c0:c1] = forcing[R:] - dot(left, tall(z1))
+
+    def finish(level):
+        w = (levels - level) * R
+        zb = z_base[level]
+        stacked = wide(j_ref[...])
+        for c0, c1 in chunks(0, w):
+            f_ref[R:, c0:c1] = dot(stacked, tall(f_ref[R:, c0:c1]))
+            value = f_ref[:, c0:c1]
+            zt_ref[:, zb + c0 : zb + c1] = tall(value)
+            zl_ref[zb + c0 : zb + c1, :] = wide(value.T)
+
+    def update(level, row):
+        part = row - level + 1
+        message(level, part).wait_recv()
+        c0, c1 = span(level, part)
+        n0 = width_of(level + 1, row, levels)
+        zb = z_base[level]
+        shift = (row - level - 1) * R
+        left = zl_ref[zb + shift : zb + shift + R, :]
+        for d0, d1 in chunks(0, c1 - c0):
+            value = own(level, c0 + d0, c0 + d1)[...] + sib(level, c0 + d0, c0 + d1)[...]
+            value = value - dot(left, zt_ref[:, zb + shift + d0 : zb + shift + d1])
+            own(level + 1, n0 + d0, n0 + d1)[...] = value
+        if row == level + 1:
+            message(level + 1, 0).start()
+            message(level + 1, 1).start()
+        else:
+            message(level + 1, row - level).start()
+
+    def gains(level):
+        mine, _ = side_slices(level)
+        e_own = e_ref[level, mine, :]
+        w1 = dot3(e_own[:, :R], inv_ref[...].T)
+        w2 = dot3(e_own[:, R:] - dot3(w1, u_ref[...]), j_ref[...].T)
+        w = wide(jnp.concatenate([w1, w2], axis=1))
+        zb = z_base[level]
+        for c0, c1 in chunks(0, (levels - level) * R):
+            g_ref[:, zb + c0 : zb + c1] = dot(w, zt_ref[:, zb + c0 : zb + c1])
+
+    barrier = pltpu.get_barrier_semaphore()
+    for device in partner:
+        pl.semaphore_signal(barrier, inc=1, device_id=device, device_id_type=pl.DeviceIdType.MESH)
+    pl.semaphore_wait(barrier, levels)
+    for part in range(levels + 1):
+        message(0, part).start()
+    prepare(0)
+    begin(0)
+
+    late = {
+        (1, 0): [(0, 2)],
+        (1, 1): [(0, 3)],
+        (2, 0): [(0, 4), (0, 5)],
+        (2, 1): [(0, 6), (1, 3)],
+        (3, 0): [(1, 4), (1, 5), (1, 6), (2, 4)],
+        (4, 0): [(2, 5), (2, 6), (3, 5), (3, 6)],
+        (5, 0): [(4, 6)],
+    }
+
+    def step(i, carry):
+        factor(a_ref, j_ref)
+        for level in range(levels):
+
+            @pl.when(i == 2 * level)
+            def _(level=level):
+                half(level)
+                for pair in late.get((level, 0), []):
+                    update(*pair)
+
+            @pl.when(i == 2 * level + 1)
+            def _(level=level):
+                finish(level)
+                for pair in late.get((level, 1), []):
+                    update(*pair)
+                if level < levels - 1:
+                    update(level, level + 1)
+                    prepare(level + 1)
+                gains(level)
+                if level < levels - 1:
+                    begin(level + 1)
+
+        return carry
+
+    lax.fori_loop(0, 2 * levels, step, 0)
+    for level in range(levels):
+        for part in range(levels + 1 - level):
+            message(level, part).wait_send()
+
+
+def final_kernel(y_ref, u_ref, li_ref, g_ref, out_ref, v_ref, x_ref):
+    levels = y_ref.shape[1] // R - 1
     slots = y_ref.shape[0]
     nb = slots // R
     for k in reversed(range(levels)):
-        g = g_refs[k]
-        value = -g[:, g.shape[1] - R :]
-        if k < levels - 1:
-            value = value - dot3(g[:, : g.shape[1] - R], v_ref[(k + 1) * R :, :])
+        base = sum((levels - j) * R for j in range(k))
+        inner = (levels - 1 - k) * R
+        value = -g_ref[:, base + inner : base + inner + R]
+        if inner > 0:
+            value = value - dot3(g_ref[:, base : base + inner], v_ref[(k + 1) * R :, :])
         v_ref[blk(k), :] = value
     vt = tall(v_ref[...])
     for b in range(nb):
@@ -267,14 +385,14 @@
     return jax.ShapeDtypeStruct(shape, F32)
 
 
-def call(kernel, outs, ins, scratch=(), **kw):
+def call(kernel, outs, ins, scratch=(), params=PARAMS, **kw):
     return pl.pallas_call(
         kernel,
         out_shape=outs,
         in_specs=ins,
         out_specs=jax.tree.map(lambda _: VMEM, outs),
         scratch_shapes=list(scratch),
-        compiler_params=PARAMS,
+        compiler_params=params,
         **kw,
     )
 
@@ -284,10 +402,10 @@
     levels = basis.shape[1] // R
     columns = levels * R + right_side.shape[1]
     ordered = points[:, order[0]]
-    trail_width = sum(columns - k * R for k in range(1, levels))
-    row, trail, y, u, li = call(
+    packed = width_of(0, levels, levels)
+    t, y, u, li = call(
         leaf_kernel,
-        (f32(R, columns), f32(R, trail_width), f32(slots, columns), f32(slots, slots), f32(slots, R)),
+        (f32(R, packed), f32(slots, columns), f32(slots, slots), f32(slots, R)),
         [SMEM, VMEM, VMEM, VMEM, VMEM],
         [
             pltpu.VMEM((R, R), F32),
@@ -298,47 +416,40 @@
             pltpu.VMEM((slots, columns), BF16),
         ],
     )(counts, ordered, ordered.T, basis, right_side)
-    subs = lax.axis_size("sub")
-    sub_bits = subs.bit_length() - 1
-    position = lax.axis_index("leaf") * subs + lax.axis_index("sub")
-    neighbour = {0: ("sub", 1), 1: ("sub", 3), 2: ("leaf", 1), 3: ("leaf", 2), 4: ("leaf", 6), 5: ("leaf", 8), 6: ("leaf", 24)}
-
-    def swap(x, level):
-        axis, mask = neighbour[level]
-        return lax.ppermute(x, axis, [(i, i ^ mask) for i in range(lax.axis_size(axis))])
-
-    gs = []
-    for level in range(levels):
-        last = level == levels - 1
-        width = columns - (level + 1) * R
-        sib = swap(row, level)
-        if not last:
-            sib_trail = swap(trail, level)
-        side = (position >> level & 1).reshape(1)
-        z, w = call(
-            level_kernel,
-            (f32(2 * R, width), f32(R, 2 * R)),
-            [VMEM, VMEM, VMEM, SMEM],
-            [pltpu.VMEM((2 * R, width + R), F32), pltpu.VMEM((R, R), F32), pltpu.VMEM((R, R), F32)],
-            cost_estimate=pl.CostEstimate(flops=20_000_000_000, bytes_accessed=4_000_000, transcendentals=0),
-        )(row, sib, coupling[level], side)
-        if last:
-            gs.append(call(g_kernel, f32(R, width), [VMEM, VMEM])(z, w))
-        else:
-            row = call(next_row_kernel, f32(R, width), [VMEM] * 3)(trail, sib_trail, z)
-            if level < levels - 2:
-                trail, g = call(rest_kernel, (f32(R, trail.shape[1] - width), f32(R, width)), [VMEM] * 4)(
-                    trail, sib_trail, z, w
-                )
-            else:
-                g = call(g_kernel, f32(R, width), [VMEM, VMEM])(z, w)
-            gs.append(g)
+    own_width = sum(width_of(k, levels, levels) for k in range(1, levels))
+    gain_width = sum((levels - k) * R for k in range(levels))
+    messages = sum(levels + 1 - k for k in range(levels))
+    g = call(
+        functools.partial(levels_kernel, levels),
+        f32(R, gain_width),
+        [VMEM, VMEM],
+        [
+            pltpu.VMEM((R, own_width), F32),
+            pltpu.VMEM((R, own_width + packed), F32),
+            pltpu.VMEM((6 * R, gain_width), BF16),
+            pltpu.VMEM((gain_width, 6 * R), BF16),
+            pltpu.VMEM((2 * R, 2 * R), F32),
+            pltpu.VMEM((2 * R, R), F32),
+            pltpu.VMEM((2 * R, levels * R), F32),
+            pltpu.VMEM((2 * R, 6 * R), BF16),
+            pltpu.VMEM((6 * R, 2 * R), BF16),
+            pltpu.VMEM((R, R), F32),
+            pltpu.VMEM((R, R), F32),
+            pltpu.VMEM((R, R), F32),
+            pltpu.VMEM((R, R), F32),
+            pltpu.SemaphoreType.DMA((messages,)),
+            pltpu.SemaphoreType.DMA((messages,)),
+        ],
+        pltpu.CompilerParams(
+            vmem_limit_bytes=56 * 1024 * 1024, collective_id=0, has_side_effects=True
+        ),
+    )(t, coupling)
     return call(
         final_kernel,
         f32(slots, columns - levels * R),
-        [VMEM] * (3 + levels),
+        [VMEM] * 4,
         [pltpu.VMEM((levels * R, R), F32), pltpu.VMEM((slots, R), F32)],
-    )(y, u, li, *gs)
+    )(y, u, li, g)
 
 
 def solution(mesh):

time: 291 us -> 217 us (0.75)
  waiting for transfers between devices: 66 us -> 0 us
  Pallas kernels: 184 us -> 208 us
  starting transfers between devices: 18.4 us -> 0 us
  local copies, waits for them, and re-layouts: 17.8 us -> 4.54 us
    ppermute x13 -> x0, waiting for transfers between devices: 66 us -> none  [swap(): lax.ppermute(x, axis, [(i, i ^ mask) for i in range(lax.axis_size(axis))])]
    pallas_call x22 -> x3, Pallas kernels: 184 us -> 208 us  [the longest x1 145 us: shards(): call(functools.partial(levels_kernel, levels), f32(R, gain_width), [VMEM,...]
    ppermute x13 -> x0, starting transfers between devices: 18.4 us -> none  [swap(): lax.ppermute(x, axis, [(i, i ^ mask) for i in range(lax.axis_size(axis))])]
    unnamed x29 -> x3, local copies, waits for them, and re-layouts: 11.5 us -> 0.94 us
  transfers between devices with their start and end apart: 13 -> 0, of which waited for: 8 -> 0; matrix products, arithmetic and copies ran while one was open for 1% -> 0% of each run, Pallas kernels for 32% -> 0%
where the time goes in v2:
time: 217 us; the launch traced here: 214 us
  Pallas kernels  208 us (96%)
  local copies, waits for them, and re-layouts  4.54 us (2%)
    pallas_call x1, Pallas kernels, shards(): call(functools.partial(levels_kernel, levels), f32(R, gain_width), [VMEM,...  145 us
    pallas_call x1, Pallas kernels, shards(): call(leaf_kernel, (f32(R, packed), f32(slots, columns), f32(slots, slots)...  51.9 us
    pallas_call x1, Pallas kernels, shards(): call(final_kernel, f32(slots, columns - levels * R), [VMEM] * 4, [pltpu.V...  11.2 us

profile of v2, /device:TPU:0, one launch (start us, length us, event | category | flops | bytes accessed | tf_op | source)
XLA Modules:
  0.0 214.2 jit_solution(14265282704506342403)
XLA Ops:
  0.7 0.7 compare_select_fusion
  1.4 0.9 copy.9
  2.3 2.8 %gather_fusion = f32[1024,3]{1,0:T(8,128)S(1)} fusion(f32[3,1024]{0,1:T(8,128)S(1)} %copy.9, s32[1024]{0:T(1024)S(1)} %broadcast_clamp_fusion), kind=kCustom, calls=%fused_computation | custom fusion | bytes 28672 | tf_op jit(solution)/shard_map/gather | solution.py:404
  5.1 0.0 copy-start
  5.1 0.8 copy.10
  5.9 0.0 copy-done
  5.9 51.9 %shard_map.64 = (f32[128,4480]{1,0:T(8,128)}, f32[1024,1024]{1,0:T(8,128)}, f32[1024,1024]{1,0:T(8,128)}, f32[1024,128]{1,0:T(8,128)}) custom-call(s32[1]{0:T(128)S(6)} %copy.11.count_ref, f32[3,1024]{1,0:T(4,128)} %bitcast.4, f32[1024,3]{1,0:T(8,128)} %copy-done, f32[1024,896]{1,0:T(8,128)} %basis_ref.1, f32[1024,128]{1,0:T(8,128)} %rhs_ref.1), custom_call_target="tpu_custom_call" | custom-call | tf_op jit(solution)/shard_map/pallas_call | solution.py:406
  57.8 144.9 %shard_map.65.g_ref = f32[128,3584]{1,0:T(8,128)} custom-call(f32[128,4480]{1,0:T(8,128)} %get-tuple-element.12.t_ref, f32[7,256,256]{2,1,0:T(8,128)} %e_ref.1), custom_call_target="tpu_custom_call" | custom-call | tf_op jit(solution)/shard_map/pallas_call | solution.py:422
  202.8 11.2 %shard_map.66 = f32[1024,128]{1,0:T(8,128)} custom-call(f32[1024,1024]{1,0:T(8,128)} %get-tuple-element.9.y_ref, f32[1024,1024]{1,0:T(8,128)} %get-tuple-element.10.u_ref, f32[1024,128]{1,0:T(8,128)} %get-tuple-element.11.li_ref, f32[128,3584]{1,0:T(8,128)} %shard_map.65.g_ref), custom_call_target="tpu_custom_call" | custom-call | tf_op jit(solution)/shard_map/pallas_call | solution.py:447
  (1 shorter events, 0.0 us)
Async XLA Ops:
  5.1 0.8 copy-start

commit v3 on v2

--- a/solution.py
+++ b/solution.py
@@ -50,16 +50,28 @@
 def factor(a_ref, j_ref):
     n = R
     groups = n // 8
-    j_ref[...] = identity(n)
     sub = lax.broadcasted_iota(jnp.int32, (8, n), 0)
+    lane = lax.broadcasted_iota(jnp.int32, (8, n), 1)
+    rows = [a_ref[8 * g : 8 * g + 8, :] for g in range(groups)]
+
+    def column(x, c):
+        return jnp.take_along_axis(x, jnp.full((8, n), c, jnp.int32), axis=1, mode="promise_in_bounds")
+
+    def row(x, r):
+        return jnp.broadcast_to(x[r : r + 1, :], (8, n))
+
     for p in range(groups):
         r0 = 8 * p
-        panel = a_ref[r0 : r0 + 8, :]
-        eye_p = j_ref[r0 : r0 + 8, :]
-        cols = [jnp.broadcast_to(panel[:, r0 + c : r0 + c + 1], (8, n)) for c in range(8)]
-        a = [[jnp.broadcast_to(cols[c][s : s + 1, :], (8, n)) for c in range(s + 1)] for s in range(8)]
+        inside = (lane >= r0) & (lane < r0 + 8)
+        cols = [column(rows[p], r0 + c) for c in range(8)]
+        a = [[row(cols[c], s) for c in range(s + 1)] for s in range(8)]
+        panel = jnp.where(inside, (sub == lane - r0).astype(F32), rows[p])
         rs = [None] * 8
         low = [[None] * 8 for _ in range(8)]
+        up = [row(panel, r) for r in range(8)]
+        later = range(p + 1, groups)
+        m = {g: [column(rows[g], r0 + r) for r in range(8)] for g in later}
+        acc = {g: jnp.where(inside, 0.0, rows[g]) for g in later}
         for r in range(8):
             rs[r] = lax.rsqrt(a[r][r])
             for s in range(r + 1, 8):
@@ -67,34 +79,20 @@
             for s in range(r + 1, 8):
                 for c in range(r + 1, s + 1):
                     a[s][c] = a[s][c] - low[s][r] * low[c][r]
-        urow = []
-        jrow = []
-        for r in range(8):
-            ur = jnp.broadcast_to(panel[r : r + 1, :], (8, n))
-            jr = jnp.broadcast_to(eye_p[r : r + 1, :], (8, n))
-            for k in range(r):
-                ur = ur - low[r][k] * urow[k]
-                jr = jr - low[r][k] * jrow[k]
-            urow.append(ur * rs[r])
-            jrow.append(jr * rs[r])
-        done = jrow[0]
+            up[r] = up[r] * rs[r]
+            for s in range(r + 1, 8):
+                up[s] = up[s] - low[s][r] * up[r]
+            for g in later:
+                m[g][r] = m[g][r] * rs[r]
+                for s in range(r + 1, 8):
+                    m[g][s] = m[g][s] - low[s][r] * m[g][r]
+                acc[g] = acc[g] - m[g][r] * up[r]
+        for g in later:
+            rows[g] = acc[g]
+        done = up[0]
         for r in range(1, 8):
-            done = jnp.where(sub == r, jrow[r], done)
-        j_ref[r0 : r0 + 8, :] = done
-        for g in range(p + 1, groups):
-            ag = a_ref[8 * g : 8 * g + 8, :]
-            jg = j_ref[8 * g : 8 * g + 8, :]
-            acc_a, acc_j = ag, jg
-            m = []
-            for r in range(8):
-                b = jnp.broadcast_to(ag[:, r0 + r : r0 + r + 1], (8, n))
-                for k in range(r):
-                    b = b - low[r][k] * m[k]
-                m.append(b * rs[r])
-                acc_a = acc_a - m[r] * urow[r]
-                acc_j = acc_j - m[r] * jrow[r]
-            a_ref[8 * g : 8 * g + 8, :] = acc_a
-            j_ref[8 * g : 8 * g + 8, :] = acc_j
+            done = jnp.where(sub == r, up[r], done)
+        j_ref[r0 : r0 + 8, :] = jnp.where(lane < r0 + 8, done, 0.0)
 
 
 def chunks(start, stop, size=256):

time: 217 us -> 202 us (0.931)
  Pallas kernels: 208 us -> 193 us
    pallas_call x1, Pallas kernels: 51.9 us -> 44 us  [shards(): call(leaf_kernel, (f32(R, packed), f32(slots, columns), f32(slots, slots)...]
    pallas_call x1, Pallas kernels: 145 us -> 138 us  [shards(): call(functools.partial(levels_kernel, levels), f32(R, gain_width), [VMEM,...]
where the time goes in v3:
time: 202 us; the launch traced here: 199 us
  Pallas kernels  193 us (96%)
  local copies, waits for them, and re-layouts  4.54 us (2%)
    pallas_call x1, Pallas kernels, shards(): call(functools.partial(levels_kernel, levels), f32(R, gain_width), [VMEM,...  138 us
    pallas_call x1, Pallas kernels, shards(): call(leaf_kernel, (f32(R, packed), f32(slots, columns), f32(slots, slots)...  44 us
    pallas_call x1, Pallas kernels, shards(): call(final_kernel, f32(slots, columns - levels * R), [VMEM] * 4, [pltpu.V...  11.2 us

profile of v3, /device:TPU:0, one launch (start us, length us, event | category | flops | bytes accessed | tf_op | source)
XLA Modules:
  0.0 199.1 jit_solution(13638782244005744698)
XLA Ops:
  0.7 0.7 compare_select_fusion
  1.4 0.9 copy.9
  2.3 2.8 %gather_fusion = f32[1024,3]{1,0:T(8,128)S(1)} fusion(f32[3,1024]{0,1:T(8,128)S(1)} %copy.9, s32[1024]{0:T(1024)S(1)} %broadcast_clamp_fusion), kind=kCustom, calls=%fused_computation | custom fusion | bytes 28672 | tf_op jit(solution)/shard_map/gather | solution.py:402
  5.1 0.0 copy-start
  5.1 0.8 copy.10
  5.9 0.0 copy-done
  5.9 44.0 %shard_map.64 = (f32[128,4480]{1,0:T(8,128)}, f32[1024,1024]{1,0:T(8,128)}, f32[1024,1024]{1,0:T(8,128)}, f32[1024,128]{1,0:T(8,128)}) custom-call(s32[1]{0:T(128)S(6)} %copy.11.count_ref, f32[3,1024]{1,0:T(4,128)} %bitcast.4, f32[1024,3]{1,0:T(8,128)} %copy-done, f32[1024,896]{1,0:T(8,128)} %basis_ref.1, f32[1024,128]{1,0:T(8,128)} %rhs_ref.1), custom_call_target="tpu_custom_call" | custom-call | tf_op jit(solution)/shard_map/pallas_call | solution.py:404
  49.9 137.8 %shard_map.65.g_ref = f32[128,3584]{1,0:T(8,128)} custom-call(f32[128,4480]{1,0:T(8,128)} %get-tuple-element.12.t_ref, f32[7,256,256]{2,1,0:T(8,128)} %e_ref.1), custom_call_target="tpu_custom_call" | custom-call | tf_op jit(solution)/shard_map/pallas_call | solution.py:420
  187.7 11.2 %shard_map.66 = f32[1024,128]{1,0:T(8,128)} custom-call(f32[1024,1024]{1,0:T(8,128)} %get-tuple-element.9.y_ref, f32[1024,1024]{1,0:T(8,128)} %get-tuple-element.10.u_ref, f32[1024,128]{1,0:T(8,128)} %get-tuple-element.11.li_ref, f32[128,3584]{1,0:T(8,128)} %shard_map.65.g_ref), custom_call_target="tpu_custom_call" | custom-call | tf_op jit(solution)/shard_map/pallas_call | solution.py:445
  (1 shorter events, 0.0 us)
Async XLA Ops:
  5.1 0.8 copy-start

commit v4 on v3

--- a/solution.py
+++ b/solution.py
@@ -104,14 +104,25 @@
 
 
 def leaf_kernel(
-    count_ref, xr_ref, xc_ref, basis_ref, rhs_ref,
+    count_ref, points_ref, order_ref, basis_ref, rhs_ref,
     t_ref, y_ref, u_ref, li_ref,
-    a_ref, j_ref, right_ref, left_ref, yh_ref, yl_ref,
+    a_ref, j_ref, right_ref, left_ref, yh_ref, yl_ref, xr_ref, xc_ref,
 ):
     slots, columns = y_ref.shape
     nb = slots // R
     levels = basis_ref.shape[1] // R
     count = count_ref[0]
+    points = points_ref[...]
+    high = points.astype(BF16)
+    middle = (points - high.astype(F32)).astype(BF16)
+    low = (points - high.astype(F32) - middle.astype(F32)).astype(BF16)
+    xr_ref[...] = jnp.zeros_like(xr_ref)
+    source = lax.broadcasted_iota(jnp.int32, (slots, 256), 0)
+    for c0, c1 in chunks(0, slots, 256):
+        chosen = (source == order_ref[:, c0:c1]).astype(F32).astype(BF16)
+        xr_ref[:3, c0:c1] = dot(high, chosen) + dot(middle, chosen) + dot(low, chosen)
+    for b in range(nb):
+        xc_ref[blk(b), :] = xr_ref[:, blk(b)].T
     live_lane = (lax.broadcasted_iota(jnp.int32, (1, slots), 1) < count).astype(F32)
     live_sub = (lax.broadcasted_iota(jnp.int32, (slots, 1), 0) < count).astype(F32)
     for b in range(nb):
@@ -313,20 +324,21 @@
     for device in partner:
         pl.semaphore_signal(barrier, inc=1, device_id=device, device_id_type=pl.DeviceIdType.MESH)
     pl.semaphore_wait(barrier, levels)
-    for part in range(levels + 1):
-        message(0, part).start()
+    message(0, 0).start()
+    message(0, 1).start()
     prepare(0)
     begin(0)
 
-    late = {
-        (1, 0): [(0, 2)],
-        (1, 1): [(0, 3)],
-        (2, 0): [(0, 4), (0, 5)],
-        (2, 1): [(0, 6), (1, 3)],
-        (3, 0): [(1, 4), (1, 5), (1, 6), (2, 4)],
-        (4, 0): [(2, 5), (2, 6), (3, 5), (3, 6)],
+    starts = {(0, 0): [2], (0, 1): [3], (1, 0): [4], (1, 1): [5, 6, 7]}
+    ahead = {(1, 0): [(0, 2)], (3, 0): [(2, 4)]}
+    after = {
+        (2, 0): [(0, 4)],
+        (2, 1): [(1, 3), (0, 5), (0, 6)],
+        (3, 0): [(1, 5), (1, 6)],
+        (4, 0): [(3, 5), (3, 6)],
         (5, 0): [(4, 6)],
     }
+    then = {(1, 1): [(0, 3)], (2, 1): [(1, 4)], (3, 1): [(2, 5), (2, 6)]}
 
     def step(i, carry):
         factor(a_ref, j_ref)
@@ -334,17 +346,25 @@
 
             @pl.when(i == 2 * level)
             def _(level=level):
+                for part in starts.get((level, 0), []):
+                    message(0, part).start()
+                for pair in ahead.get((level, 0), []):
+                    update(*pair)
                 half(level)
-                for pair in late.get((level, 0), []):
+                for pair in after.get((level, 0), []):
                     update(*pair)
 
             @pl.when(i == 2 * level + 1)
             def _(level=level):
+                for part in starts.get((level, 1), []):
+                    message(0, part).start()
                 finish(level)
-                for pair in late.get((level, 1), []):
+                for pair in after.get((level, 1), []):
                     update(*pair)
                 if level < levels - 1:
                     update(level, level + 1)
+                    for pair in then.get((level, 1), []):
+                        update(*pair)
                     prepare(level + 1)
                 gains(level)
                 if level < levels - 1:
@@ -399,7 +419,6 @@
     slots = points.shape[1]
     levels = basis.shape[1] // R
     columns = levels * R + right_side.shape[1]
-    ordered = points[:, order[0]]
     packed = width_of(0, levels, levels)
     t, y, u, li = call(
         leaf_kernel,
@@ -412,8 +431,10 @@
             pltpu.VMEM((slots, 3 * R), BF16),
             pltpu.VMEM((slots, columns), BF16),
             pltpu.VMEM((slots, columns), BF16),
+            pltpu.VMEM((8, slots), F32),
+            pltpu.VMEM((slots, 8), F32),
         ],
-    )(counts, ordered, ordered.T, basis, right_side)
+    )(counts, points, order, basis, right_side)
     own_width = sum(width_of(k, levels, levels) for k in range(1, levels))
     gain_width = sum((levels - k) * R for k in range(levels))
     messages = sum(levels + 1 - k for k in range(levels))

time: 202 us -> 182 us (0.901)
  Pallas kernels: 193 us -> 179 us
  local copies, waits for them, and re-layouts: 4.54 us -> 0 us
    pallas_call x1, Pallas kernels: 138 us -> 122 us  [shards(): call(functools.partial(levels_kernel, levels), f32(R, gain_width), [VMEM,...]
    gather x2 -> x0, local copies, waits for them, and re-layouts: 3.6 us -> none  [shards(): ordered = points[:, order[0]]]
where the time goes in v4:
time: 182 us; the launch traced here: 179 us
  Pallas kernels  179 us (98%)
    pallas_call x1, Pallas kernels, shards(): call(functools.partial(levels_kernel, levels), f32(R, gain_width), [VMEM,...  122 us
    pallas_call x1, Pallas kernels, shards(): call(leaf_kernel, (f32(R, packed), f32(slots, columns), f32(slots, slots)...  45.3 us
    pallas_call x1, Pallas kernels, shards(): call(final_kernel, f32(slots, columns - levels * R), [VMEM] * 4, [pltpu.V...  11.2 us

profile of v4, /device:TPU:0, one launch (start us, length us, event | category | flops | bytes accessed | tf_op | source)
XLA Modules:
  0.0 179.4 jit_solution(5361134206626288421)
XLA Ops:
  0.7 45.3 %shard_map.64 = (f32[128,4480]{1,0:T(8,128)}, f32[1024,1024]{1,0:T(8,128)}, f32[1024,1024]{1,0:T(8,128)}, f32[1024,128]{1,0:T(8,128)}) custom-call(s32[1]{0:T(128)S(6)} %copy.7.count_ref, f32[3,1024]{1,0:T(4,128)} %points_ref.1, s32[1,1024]{1,0:T(1,128)} %order_ref.1, f32[1024,896]{1,0:T(8,128)} %basis_ref.1, f32[1024,128]{1,0:T(8,128)} %rhs_ref.1), custom_call_target="tpu_custom_call" | custom-call | tf_op jit(solution)/shard_map/pallas_call | solution.py:423
  45.9 122.1 %shard_map.65.g_ref = f32[128,3584]{1,0:T(8,128)} custom-call(f32[128,4480]{1,0:T(8,128)} %get-tuple-element.12.t_ref, f32[7,256,256]{2,1,0:T(8,128)} %e_ref.1), custom_call_target="tpu_custom_call" | custom-call | tf_op jit(solution)/shard_map/pallas_call | solution.py:441
  168.0 11.2 %shard_map.66 = f32[1024,128]{1,0:T(8,128)} custom-call(f32[1024,1024]{1,0:T(8,128)} %get-tuple-element.9.y_ref, f32[1024,1024]{1,0:T(8,128)} %get-tuple-element.10.u_ref, f32[1024,128]{1,0:T(8,128)} %get-tuple-element.11.li_ref, f32[128,3584]{1,0:T(8,128)} %shard_map.65.g_ref), custom_call_target="tpu_custom_call" | custom-call | tf_op jit(solution)/shard_map/pallas_call | solution.py:466

commit v5 on v4

--- a/solution.py
+++ b/solution.py
@@ -14,6 +14,7 @@
 BF16 = jnp.bfloat16
 VMEM = pl.BlockSpec(memory_space=pltpu.VMEM)
 SMEM = pl.BlockSpec(memory_space=pltpu.SMEM)
+ANY = pl.BlockSpec(memory_space=pl.ANY)
 PARAMS = pltpu.CompilerParams(vmem_limit_bytes=56 * 1024 * 1024)
 
 
@@ -174,14 +175,16 @@
         return carry
 
     lax.fori_loop(0, nb, step, 0)
-    offset = 0
-    for k in range(levels):
-        high, low = split(y_ref[:, blk(k)].T)
-        for c0, c1 in chunks(k * R, columns, 256):
-            yh = yh_ref[:, c0:c1]
-            value = dot(high, yh) + dot(high, yl_ref[:, c0:c1]) + dot(low, yh)
-            t_ref[:, offset + c0 - k * R : offset + c1 - k * R] = value
-        offset += columns - k * R
+    project(0, 0, y_ref, yh_ref, yl_ref, t_ref)
+
+
+def project(k, offset, y_ref, yh_ref, yl_ref, t_ref):
+    columns = y_ref.shape[1]
+    high, low = split(y_ref[:, blk(k)].T)
+    for c0, c1 in chunks(k * R, columns, 256):
+        yh = yh_ref[:, c0:c1]
+        value = dot(high, yh) + dot(high, yl_ref[:, c0:c1]) + dot(low, yh)
+        t_ref[:, offset + c0 - k * R : offset + c1 - k * R] = value
 
 
 def width_of(level, row, levels):
@@ -189,10 +192,13 @@
 
 
 def levels_kernel(
-    levels, t_ref, e_ref, g_ref,
-    own_ref, sib_ref, zt_ref, zl_ref, bd_ref, h_ref, f_ref, eb_ref, et_ref, u_ref, inv_ref, a_ref, j_ref,
-    send_sem, recv_sem,
+    levels, row_ref, y_hbm, e_ref, g_ref,
+    t_ref, y_ref, yh_ref, yl_ref, own_ref, sib_ref, zt_ref, zl_ref, bd_ref, h_ref, f_ref, eb_ref, et_ref, u_ref, inv_ref, a_ref, j_ref,
+    send_sem, recv_sem, y_sem,
 ):
+    fetch = pltpu.make_async_copy(y_hbm, y_ref, y_sem)
+    fetch.start()
+    row_width = row_ref.shape[1]
     leaf, sub = lax.axis_index("leaf"), lax.axis_index("sub")
     core, z, y = leaf % 2, (leaf // 2) % 4, leaf // 8
     partner = [
@@ -218,8 +224,11 @@
         return start, width_of(level, level + part, levels) if part > 1 else width_of(level, level + 1, levels)
 
     def own(level, c0, c1):
-        ref = t_ref if level == 0 else own_ref
-        return ref.at[:, own_base[level] + c0 : own_base[level] + c1]
+        if level == 0:
+            if c1 <= row_width:
+                return row_ref.at[:, c0:c1]
+            return t_ref.at[:, c0 - row_width : c1 - row_width]
+        return own_ref.at[:, own_base[level] + c0 : own_base[level] + c1]
 
     def sib(level, c0, c1):
         return sib_ref.at[:, sib_base[level] + c0 : sib_base[level] + c1]
@@ -327,6 +336,13 @@
     message(0, 0).start()
     message(0, 1).start()
     prepare(0)
+    fetch.wait()
+    for b in range(y_ref.shape[0] // R):
+        high, low = split(y_ref[blk(b), :])
+        yh_ref[blk(b), :] = high
+        yl_ref[blk(b), :] = low
+    for k in range(1, levels):
+        project(k, width_of(0, k, levels) - row_width, y_ref, yh_ref, yl_ref, t_ref)
     begin(0)
 
     starts = {(0, 0): [2], (0, 1): [3], (1, 0): [4], (1, 1): [5, 6, 7]}
@@ -378,7 +394,13 @@
             message(level, part).wait_send()
 
 
-def final_kernel(y_ref, u_ref, li_ref, g_ref, out_ref, v_ref, x_ref):
+def final_kernel(y_hbm, u_hbm, li_hbm, g_ref, out_ref, y_ref, u_ref, li_ref, v_ref, x_ref, sems):
+    fetches = [
+        pltpu.make_async_copy(source, target, sems.at[i])
+        for i, (source, target) in enumerate([(y_hbm, y_ref), (li_hbm, li_ref), (u_hbm, u_ref)])
+    ]
+    for fetch in fetches:
+        fetch.start()
     levels = y_ref.shape[1] // R - 1
     slots = y_ref.shape[0]
     nb = slots // R
@@ -390,8 +412,11 @@
             value = value - dot3(g_ref[:, base : base + inner], v_ref[(k + 1) * R :, :])
         v_ref[blk(k), :] = value
     vt = tall(v_ref[...])
+    fetches[0].wait()
     for b in range(nb):
         x_ref[blk(b), :] = y_ref[blk(b), levels * R :] + dot(wide(y_ref[blk(b), : levels * R]), vt)
+    fetches[1].wait()
+    fetches[2].wait()
     for b in reversed(range(nb)):
         value = dot3(li_ref[blk(b), :].T, x_ref[blk(b), :])
         out_ref[blk(b), :] = value
@@ -422,7 +447,7 @@
     packed = width_of(0, levels, levels)
     t, y, u, li = call(
         leaf_kernel,
-        (f32(R, packed), f32(slots, columns), f32(slots, slots), f32(slots, R)),
+        (f32(R, columns), f32(slots, columns), f32(slots, slots), f32(slots, R)),
         [SMEM, VMEM, VMEM, VMEM, VMEM],
         [
             pltpu.VMEM((R, R), F32),
@@ -441,8 +466,12 @@
     g = call(
         functools.partial(levels_kernel, levels),
         f32(R, gain_width),
-        [VMEM, VMEM],
+        [VMEM, ANY, VMEM],
         [
+            pltpu.VMEM((R, packed - columns), F32),
+            pltpu.VMEM((slots, columns), F32),
+            pltpu.VMEM((slots, columns), BF16),
+            pltpu.VMEM((slots, columns), BF16),
             pltpu.VMEM((R, own_width), F32),
             pltpu.VMEM((R, own_width + packed), F32),
             pltpu.VMEM((6 * R, gain_width), BF16),
@@ -458,16 +487,24 @@
             pltpu.VMEM((R, R), F32),
             pltpu.SemaphoreType.DMA((messages,)),
             pltpu.SemaphoreType.DMA((messages,)),
+            pltpu.SemaphoreType.DMA,
         ],
         pltpu.CompilerParams(
             vmem_limit_bytes=56 * 1024 * 1024, collective_id=0, has_side_effects=True
         ),
-    )(t, coupling)
+    )(t, y, coupling)
     return call(
         final_kernel,
         f32(slots, columns - levels * R),
-        [VMEM] * 4,
-        [pltpu.VMEM((levels * R, R), F32), pltpu.VMEM((slots, R), F32)],
+        [ANY] * 3 + [VMEM],
+        [
+            pltpu.VMEM((slots, columns), F32),
+            pltpu.VMEM((slots, slots), F32),
+            pltpu.VMEM((slots, R), F32),
+            pltpu.VMEM((levels * R, R), F32),
+            pltpu.VMEM((slots, R), F32),
+            pltpu.SemaphoreType.DMA((3,)),
+        ],
     )(y, u, li, g)
 
 

time: 182 us -> 178 us (0.978)
  Pallas kernels: 179 us -> 174 us
    pallas_call x2, Pallas kernels: 56.5 us -> 52.2 us  [the longest x1 42.8 us: shards(): call(leaf_kernel, (f32(R, columns), f32(slots, columns), f32(slots, slots...]
where the time goes in v5:
time: 178 us; the launch traced here: 175 us
  Pallas kernels  174 us (98%)
    pallas_call x1, Pallas kernels, shards(): call(functools.partial(levels_kernel, levels), f32(R, gain_width), [VMEM,...  122 us
    pallas_call x1, Pallas kernels, shards(): call(leaf_kernel, (f32(R, columns), f32(slots, columns), f32(slots, slots...  42.8 us
    pallas_call x1, Pallas kernels, shards(): call(final_kernel, f32(slots, columns - levels * R), [ANY] * 3 + [VMEM],...  9.47 us

profile of v5, /device:TPU:0, one launch (start us, length us, event | category | flops | bytes accessed | tf_op | source)
XLA Modules:
  0.0 174.8 jit_solution(2174145615879575555)
XLA Ops:
  0.7 42.8 %shard_map.64 = (f32[128,1024]{1,0:T(8,128)}, f32[1024,1024]{1,0:T(8,128)}, f32[1024,1024]{1,0:T(8,128)}, f32[1024,128]{1,0:T(8,128)}) custom-call(s32[1]{0:T(128)S(6)} %copy.7.count_ref, f32[3,1024]{1,0:T(4,128)} %points_ref.1, s32[1,1024]{1,0:T(1,128)} %order_ref.1, f32[1024,896]{1,0:T(8,128)} %basis_ref.1, f32[1024,128]{1,0:T(8,128)} %rhs_ref.1), custom_call_target="tpu_custom_call" | custom-call | tf_op jit(solution)/shard_map/pallas_call | solution.py:448
  43.4 121.7 %shard_map.65.g_ref = f32[128,3584]{1,0:T(8,128)} custom-call(f32[128,1024]{1,0:T(8,128)} %get-tuple-element.12.row_ref, f32[1024,1024]{1,0:T(8,128)} %get-tuple-element.9.y_hbm, f32[7,256,256]{2,1,0:T(8,128)} %e_ref.1), custom_call_target="tpu_custom_call" | custom-call | tf_op jit(solution)/shard_map/pallas_call | solution.py:466
  165.1 9.5 %shard_map.66 = f32[1024,128]{1,0:T(8,128)} custom-call(f32[1024,1024]{1,0:T(8,128)} %get-tuple-element.9.y_hbm, f32[1024,1024]{1,0:T(8,128)} %get-tuple-element.10.u_hbm, f32[1024,128]{1,0:T(8,128)} %get-tuple-element.11.li_hbm, f32[128,3584]{1,0:T(8,128)} %shard_map.65.g_ref), custom_call_target="tpu_custom_call" | custom-call | tf_op jit(solution)/shard_map/pallas_call | solution.py:496

commit v6 on v5

--- a/solution.py
+++ b/solution.py
@@ -105,10 +105,24 @@
 
 
 def leaf_kernel(
-    count_ref, points_ref, order_ref, basis_ref, rhs_ref,
-    t_ref, y_ref, u_ref, li_ref,
-    a_ref, j_ref, right_ref, left_ref, yh_ref, yl_ref, xr_ref, xc_ref,
+    count_ref, points_ref, order_ref, basis_hbm, rhs_hbm,
+    t_ref, y_hbm, u_hbm, li_hbm, basis_ref, rhs_ref, y_ref, u_ref, li_ref,
+    a_ref, j_ref, right_ref, left_ref, yh_ref, yl_ref, xr_ref, xc_ref, in_sems, out_sems,
 ):
+    fetches = [
+        pltpu.make_async_copy(basis_hbm, basis_ref, in_sems.at[0]),
+        pltpu.make_async_copy(rhs_hbm, rhs_ref, in_sems.at[1]),
+    ]
+    for fetch in fetches:
+        fetch.start()
+
+    def stores(b):
+        return [
+            pltpu.make_async_copy(y_ref.at[blk(b), :], y_hbm.at[blk(b), :], out_sems.at[3 * b]),
+            pltpu.make_async_copy(li_ref.at[blk(b), :], li_hbm.at[blk(b), :], out_sems.at[3 * b + 1]),
+            pltpu.make_async_copy(u_ref.at[blk(b), b * R :], u_hbm.at[blk(b), b * R :], out_sems.at[3 * b + 2]),
+        ]
+
     slots, columns = y_ref.shape
     nb = slots // R
     levels = basis_ref.shape[1] // R
@@ -128,8 +142,6 @@
     live_sub = (lax.broadcasted_iota(jnp.int32, (slots, 1), 0) < count).astype(F32)
     for b in range(nb):
         live_b = live_sub[blk(b), :]
-        y_ref[blk(b), : levels * R] = basis_ref[blk(b), :] * live_b
-        y_ref[blk(b), levels * R :] = rhs_ref[blk(b), :] * live_b
         for c0, c1 in chunks(b * R, slots, 128):
             dist = None
             for d in range(3):
@@ -139,6 +151,13 @@
             if c0 == b * R:
                 kern = kern + NUGGET_VALUE * identity(R)
             u_ref[blk(b), c0:c1] = kern
+
+    for fetch in fetches:
+        fetch.wait()
+    for b in range(nb):
+        live_b = live_sub[blk(b), :]
+        y_ref[blk(b), : levels * R] = basis_ref[blk(b), :] * live_b
+        y_ref[blk(b), levels * R :] = rhs_ref[blk(b), :] * live_b
 
     def step(b, carry):
         here = pl.ds(pl.multiple_of(b * R, R), R)
@@ -171,11 +190,16 @@
                         y_ref[blk(i), c0:c1] = y_ref[blk(i), c0:c1] - dot(
                             left, right_ref[:, slots + c0 : slots + c1]
                         )
+                for store in stores(b):
+                    store.start()
 
         return carry
 
     lax.fori_loop(0, nb, step, 0)
     project(0, 0, y_ref, yh_ref, yl_ref, t_ref)
+    for b in range(nb):
+        for store in stores(b):
+            store.wait()
 
 
 def project(k, offset, y_ref, yh_ref, yl_ref, t_ref):
@@ -192,10 +216,12 @@
 
 
 def levels_kernel(
-    levels, row_ref, y_hbm, e_ref, g_ref,
-    t_ref, y_ref, yh_ref, yl_ref, own_ref, sib_ref, zt_ref, zl_ref, bd_ref, h_ref, f_ref, eb_ref, et_ref, u_ref, inv_ref, a_ref, j_ref,
-    send_sem, recv_sem, y_sem,
+    levels, row_ref, y_hbm, e_hbm, g_ref,
+    e_ref, t_ref, y_ref, yh_ref, yl_ref, own_ref, sib_ref, zt_ref, zl_ref, bd_ref, h_ref, f_ref, eb_ref, et_ref, u_ref, inv_ref, a_ref, j_ref,
+    send_sem, recv_sem, y_sem, e_sem,
 ):
+    fetch_e = pltpu.make_async_copy(e_hbm, e_ref, e_sem)
+    fetch_e.start()
     fetch = pltpu.make_async_copy(y_hbm, y_ref, y_sem)
     fetch.start()
     row_width = row_ref.shape[1]
@@ -335,6 +361,7 @@
     pl.semaphore_wait(barrier, levels)
     message(0, 0).start()
     message(0, 1).start()
+    fetch_e.wait()
     prepare(0)
     fetch.wait()
     for b in range(y_ref.shape[0] // R):
@@ -428,12 +455,12 @@
     return jax.ShapeDtypeStruct(shape, F32)
 
 
-def call(kernel, outs, ins, scratch=(), params=PARAMS, **kw):
+def call(kernel, outs, ins, scratch=(), params=PARAMS, places=None, **kw):
     return pl.pallas_call(
         kernel,
         out_shape=outs,
         in_specs=ins,
-        out_specs=jax.tree.map(lambda _: VMEM, outs),
+        out_specs=places or jax.tree.map(lambda _: VMEM, outs),
         scratch_shapes=list(scratch),
         compiler_params=params,
         **kw,
@@ -448,8 +475,13 @@
     t, y, u, li = call(
         leaf_kernel,
         (f32(R, columns), f32(slots, columns), f32(slots, slots), f32(slots, R)),
-        [SMEM, VMEM, VMEM, VMEM, VMEM],
+        [SMEM, VMEM, VMEM, ANY, ANY],
         [
+            pltpu.VMEM(basis.shape, F32),
+            pltpu.VMEM(right_side.shape, F32),
+            pltpu.VMEM((slots, columns), F32),
+            pltpu.VMEM((slots, slots), F32),
+            pltpu.VMEM((slots, R), F32),
             pltpu.VMEM((R, R), F32),
             pltpu.VMEM((R, R), F32),
             pltpu.VMEM((3 * R, slots + columns), BF16),
@@ -458,7 +490,10 @@
             pltpu.VMEM((slots, columns), BF16),
             pltpu.VMEM((8, slots), F32),
             pltpu.VMEM((slots, 8), F32),
+            pltpu.SemaphoreType.DMA((2,)),
+            pltpu.SemaphoreType.DMA((3 * slots // R,)),
         ],
+        places=(VMEM, ANY, ANY, ANY),
     )(counts, points, order, basis, right_side)
     own_width = sum(width_of(k, levels, levels) for k in range(1, levels))
     gain_width = sum((levels - k) * R for k in range(levels))
@@ -466,8 +501,9 @@
     g = call(
         functools.partial(levels_kernel, levels),
         f32(R, gain_width),
-        [VMEM, ANY, VMEM],
+        [VMEM, ANY, ANY],
         [
+            pltpu.VMEM(coupling.shape, F32),
             pltpu.VMEM((R, packed - columns), F32),
             pltpu.VMEM((slots, columns), F32),
             pltpu.VMEM((slots, columns), BF16),
@@ -488,6 +524,7 @@
             pltpu.SemaphoreType.DMA((messages,)),
             pltpu.SemaphoreType.DMA((messages,)),
             pltpu.SemaphoreType.DMA,
+            pltpu.SemaphoreType.DMA,
         ],
         pltpu.CompilerParams(
             vmem_limit_bytes=56 * 1024 * 1024, collective_id=0, has_side_effects=True

time: 178 us -> 175 us (0.983)
  Pallas kernels: 174 us -> 171 us
    pallas_call x1, Pallas kernels: 42.8 us -> 40.5 us  [shards(): call(leaf_kernel, (f32(R, columns), f32(slots, columns), f32(slots, slots...]
where the time goes in v6:
time: 175 us; the launch traced here: 172 us
  Pallas kernels  171 us (98%)
    pallas_call x1, Pallas kernels, shards(): call(functools.partial(levels_kernel, levels), f32(R, gain_width), [VMEM,...  121 us
    pallas_call x1, Pallas kernels, shards(): call(leaf_kernel, (f32(R, columns), f32(slots, columns), f32(slots, slots...  40.5 us
    pallas_call x1, Pallas kernels, shards(): call(final_kernel, f32(slots, columns - levels * R), [ANY] * 3 + [VMEM],...  9.47 us

profile of v6, /device:TPU:0, one launch (start us, length us, event | category | flops | bytes accessed | tf_op | source)
XLA Modules:
  0.0 172.0 jit_solution(14407650114974254448)
XLA Ops:
  0.7 40.5 %shard_map.64 = (f32[128,1024]{1,0:T(8,128)}, f32[1024,1024]{1,0:T(8,128)}, f32[1024,1024]{1,0:T(8,128)}, f32[1024,128]{1,0:T(8,128)}) custom-call(s32[1]{0:T(128)S(6)} %copy.7.count_ref, f32[3,1024]{1,0:T(4,128)} %points_ref.1, s32[1,1024]{1,0:T(1,128)} %order_ref.1, f32[1024,896]{1,0:T(8,128)} %basis_hbm.1, f32[1024,128]{1,0:T(8,128)} %rhs_hbm.1), custom_call_target="tpu_custom_call" | custom-call | tf_op jit(solution)/shard_map/pallas_call | solution.py:475
  41.1 121.1 %shard_map.65.g_ref = f32[128,3584]{1,0:T(8,128)} custom-call(f32[128,1024]{1,0:T(8,128)} %get-tuple-element.12.row_ref, f32[1024,1024]{1,0:T(8,128)} %get-tuple-element.9.y_hbm, f32[7,256,256]{2,1,0:T(8,128)} %e_hbm.1), custom_call_target="tpu_custom_call" | custom-call | tf_op jit(solution)/shard_map/pallas_call | solution.py:501
  162.3 9.5 %shard_map.66 = f32[1024,128]{1,0:T(8,128)} custom-call(f32[1024,1024]{1,0:T(8,128)} %get-tuple-element.9.y_hbm, f32[1024,1024]{1,0:T(8,128)} %get-tuple-element.10.u_hbm, f32[1024,128]{1,0:T(8,128)} %get-tuple-element.11.li_hbm, f32[128,3584]{1,0:T(8,128)} %shard_map.65.g_ref), custom_call_target="tpu_custom_call" | custom-call | tf_op jit(solution)/shard_map/pallas_call | solution.py:533
